TPU v7x, 128 devices: a whole 4x4x4 slice. The times are simulated.
128 devices in a mesh: rep: 16 (over y, x), tp: 8 (over z, core).
Axes of the slice: x: 4, y: 4, z: 4, core: 2. Of those that a mesh axis runs over, the one named last changes fastest.
Arguments:
- queries: bfloat16 [256, 64, 128], P('rep', 'tp'), may hold values from -8 to 8
- new_kv: bfloat16 [256, 8, 256], P('rep', 'tp'), may hold values from -6 to 6
- parent_cache: bfloat16 [128, 8, 1024, 256], P('rep', 'tp'), may hold values from -8 to 8
- parent_len: int32 [128], replicated, may hold values from 1 to 1023, as said below
- child_parent: int32 [256], replicated, may hold values from 0 to 127, as said below
- out_weight: bfloat16 [8192, 4096], P('tp'), may hold values from -0.0625 to 0.0625
Outputs:
- mixed: bfloat16 [256, 4096], P('rep', 'tp')
Inputs may be any that keep to these rules, and one draw needn't show every extreme that they name: `parent_len`: some parent has exactly 1023 positions in use. Among the 16 children of one index of rep (consecutive entries), at most 2 have parents held by any one index of rep (child_parent // 8), and on every index of rep some holder has exactly 2 of them.
All inputs are finite; a program needn't handle non-finite values.
Results may differ from a plain program's by a relative error of at most 0.0055.
Values may be sent and summed in bfloat16 or wider, within the bound.
No kernel may reach another device: no remote copies, remote signals or barrier semaphores. Data moves between devices by JAX's collectives and lax.ppermute only.
A program may use at most 128 MiB of HBM per device.

v0:
```python
import jax
import jax.numpy as jnp
from jax import lax
from jax.sharding import PartitionSpec as P

MOST = 2


def masked_scores(query_rows, blocks, lengths, reach):
    head_size = query_rows.shape[-1]
    scores = jnp.einsum(
        "bkgd,bktd->bkgt", query_rows, blocks[..., :head_size], preferred_element_type=jnp.float32
    ) * head_size ** (-0.5)
    row_ids = jnp.arange(blocks.shape[2], dtype=jnp.int32)
    visible = (row_ids[None, :] < (lengths + reach)[:, None])[:, None, None, :]
    return jnp.where(visible, scores, -jnp.inf)


def shards(queries, new_kv, parent_cache, parent_len, child_parent, out_weight):
    rep_count = lax.axis_size("rep")
    position = lax.axis_index("rep")
    parents_here, kv_here, cache_len, kv_width = parent_cache.shape
    head_size = kv_width // 2
    child_count = queries.shape[0]
    query_heads = queries.shape[1]
    group_size = query_heads // kv_here
    source = (child_parent // parents_here).reshape(rep_count, child_count)
    local_id = (child_parent % parents_here).reshape(rep_count, child_count)
    earlier = jnp.arange(child_count)[None, :] < jnp.arange(child_count)[:, None]
    order_rank = jnp.sum((source[:, :, None] == source[:, None, :]) & earlier[None], axis=2)
    slot_ids = jnp.arange(MOST, dtype=jnp.int32)
    matched = (
        (source == position)[:, :, None] & (order_rank[:, :, None] == slot_ids[None, None, :])
    ).astype(jnp.int32)
    send_index = jnp.sum(matched * local_id[:, :, None], axis=1)
    outgoing = parent_cache[send_index]
    own_source = lax.dynamic_index_in_dim(source, position, 0, keepdims=False)
    own_rank = lax.dynamic_index_in_dim(order_rank, position, 0, keepdims=False)
    own_slot = own_source * MOST + own_rank
    own_parent = lax.dynamic_slice_in_dim(child_parent, position * child_count, child_count)
    own_length = parent_len[own_parent]
    grouped = queries.reshape(child_count, kv_here, group_size, head_size)
    arrived = lax.all_to_all(outgoing, "rep", split_axis=0, concat_axis=0, tiled=True)
    inherited = arrived.reshape((rep_count * MOST,) + arrived.shape[2:])[own_slot]
    row_ids = jnp.arange(cache_len, dtype=jnp.int32)
    inherit_mask = (row_ids[None, :] < own_length[:, None])[:, None, :, None]
    fresh_mask = (row_ids[None, :] == own_length[:, None])[:, None, :, None]
    child_cache = jnp.where(
        inherit_mask,
        inherited,
        jnp.where(fresh_mask, new_kv[:, :, None, :], jnp.zeros((), parent_cache.dtype)),
    )
    scores = masked_scores(grouped, child_cache, own_length, 1)
    row_max = jnp.max(scores, axis=-1, keepdims=True)
    weights = jnp.exp(scores - row_max)
    denominator = jnp.sum(weights, axis=-1, keepdims=True)
    summed = jnp.einsum(
        "bkgt,bktd->bkgd",
        weights.astype(jnp.bfloat16),
        child_cache[..., head_size:],
        preferred_element_type=jnp.float32,
    )
    head_out = (summed / denominator).astype(jnp.bfloat16)
    partial_terms = jnp.dot(
        head_out.reshape(child_count, query_heads * head_size),
        out_weight,
        preferred_element_type=jnp.float32,
    )
    projected = lax.psum_scatter(partial_terms, "tp", scatter_dimension=1, tiled=True).astype(
        jnp.bfloat16
    )
    return projected


def solution(mesh):
    placed = (
        P("rep", "tp", None),
        P("rep", "tp", None),
        P("rep", "tp", None, None),
        P(),
        P(),
        P("tp", None),
    )
    return jax.shard_map(
        shards, mesh=mesh, in_specs=placed, out_specs=P("rep", "tp"), check_vma=False
    )
```

profile of v0, /device:TPU:1, one launch (start us, length us, event | category | flops | bytes accessed | tf_op | source)
XLA Modules:
  0.0 335.2 jit_solution(4463054130920813308)
XLA Ops:
  6.5 0.0 copy-start
  6.5 0.7 and_select_fusion.1
  7.2 0.1 reshape.185
  7.3 0.4 convert_reduce_fusion
  7.8 0.1 mul.33
  7.8 0.1 select_reduce_fusion
  8.0 0.1 copy.10
  8.1 0.1 reshape.202
  8.2 9.3 %gather_fusion.1 = bf16[32,1024,256]{2,1,0:T(8,128)(2,1)} fusion(bf16[8,1024,256]{2,1,0:T(8,128)(2,1)} %bitcast.40, s32[1024]{0:T(1024)S(1)} %pad_clamp_fusion.1), kind=kCustom, calls=%fused_computation.1 | custom fusion | bytes 33554560 | tf_op jit(solution)/shard_map/gather | solution.py:36
  17.5 0.0 copy-start.3
  17.5 0.0 copy-start.1
  17.5 7.7 %all-to-all-start = ((bf16[16,2,1,1024,256]{4,3,1,2,0:T(8,128)(2,1)}), bf16[16,2,1,1024,256]{4,3,1,2,0:T(8,128)(2,1)}, u32[]{:S(2)}, u32[]{:S(2)}) async-start(bf16[16,2,1,1024,256]{4,3,1,2,0:T(8,128)(2,1)} %bitcast.41), calls=%async_computation | async-start | bytes 33554432 | tf_op jit(solution)/shard_map/all_to_all | solution.py:43
  25.2 0.0 reduce-scatter.2.cloned.1.call-start
  25.3 0.0 copy-done.3
  25.3 0.1 compare_select_fusion.2
  25.4 0.0 copy-done.1
  25.4 0.7 gather_fusion
  26.1 0.1 iota_compare_fusion.2
  26.1 0.1 iota_compare_fusion.1
  26.2 247.8 %all-to-all-done = bf16[16,2,1,1024,256]{4,3,1,2,0:T(8,128)(2,1)} async-done(((bf16[16,2,1,1024,256]{4,3,1,2,0:T(8,128)(2,1)}), bf16[16,2,1,1024,256]{4,3,1,2,0:T(8,128)(2,1)}, u32[]{:S(2)}, u32[]{:S(2)}) %all-to-all-start) | async-done | bytes 16777248 | tf_op jit(solution)/shard_map/all_to_all | solution.py:43
  274.1 0.0 copy-start.2
  274.1 10.5 %gather_fusion.2 = bf16[16,1024,256]{2,1,0:T(8,128)(2,1)} fusion(bf16[32,1024,256]{2,1,0:T(8,128)(2,1)} %bitcast.3, s32[1024]{0:T(1024)S(1)} %pad_clamp_fusion), kind=kCustom, calls=%fused_computation.2 | custom fusion | bytes 16777280 | tf_op jit(solution)/shard_map/gather | solution.py:44
  284.6 0.0 copy-done.2
  284.6 6.8 %bitcast_select_fusion = bf16[16,1,1024,256]{3,2,0,1:T(8,128)(2,1)S(1)} fusion(bf16[16,1024,256]{2,1,0:T(8,128)(2,1)} %gather_fusion.2, pred[16,1024]{1,0:T(8,128)(4,1)S(1)} %get-tuple-element.8, pred[16,1024]{1,0:T(8,128)(4,1)S(1)} %get-tuple-element.7, bf16[16,256]{1,0:T(8,128)(2,1)S(1)} %bitcast.43), kind=kLoop, calls=%fused_computation.3 | loop fusion | flops 8388608 | bytes 16818176 | tf_op jit(solution)/shard_map/jit(_where)/select_n | solution.py:48
  291.4 0.0 copy-done
  291.4 1.3 fusion.16
  292.7 0.2 fusion.7
  292.9 0.7 fusion.6
  293.6 5.3 %fusion.11 = f32[16,4096]{1,0:T(8,128)} fusion(bf16[1024,4096]{1,0:T(8,128)(2,1)} %param.11, bf16[2,8,8,128]{3,2,1,0:T(8,128)(2,1)S(1)} %bitcast.42), kind=kOutput, calls=%fused_computation.21 | convolution fusion | flops 134217728 | bytes 8683520 | tf_op jit(solution)/shard_map/dot_general | solution.py:64
  298.9 0.0 reduce-scatter.2.cloned.1.call-update
  299.0 28.0 %reduce-scatter.2.cloned.1.call-done = f32[16,512]{1,0:T(8,128)} async-done(((f32[16,4096]{1,0:T(8,128)}), f32[16,512]{1,0:T(8,128)}) %reduce-scatter.2.cloned.1.call-update) | async-done | bytes 32784 | tf_op jit(solution)/shard_map/reduce_scatter | solution.py:69
  326.9 1.4 convert_element_type.18
  (8 shorter events, 0.1 us)
Async XLA Ops:
  6.5 284.9 %copy-start = (bf16[16,8,128]{2,1,0:T(8,128)(2,1)S(1)}, bf16[16,8,128]{2,1,0:T(8,128)(2,1)}, u32[]{:S(2)}) copy-start(bf16[16,8,128]{2,1,0:T(8,128)(2,1)} %param.6) | copy-start | bytes 98308
  17.5 7.8 %copy-start.3 = (s32[256]{0:T(256)S(1)}, s32[256]{0:T(256)}, u32[]{:S(2)}) copy-start(s32[256]{0:T(256)} %param.10) | copy-start | bytes 3076
  17.5 7.9 %copy-start.1 = (s32[128]{0:T(128)S(1)}, s32[128]{0:T(128)}, u32[]{:S(2)}) copy-start(s32[128]{0:T(128)} %param.9) | copy-start | bytes 1540
  17.5 256.6 %all-to-all-start = ((bf16[16,2,1,1024,256]{4,3,1,2,0:T(8,128)(2,1)}), bf16[16,2,1,1024,256]{4,3,1,2,0:T(8,128)(2,1)}, u32[]{:S(2)}, u32[]{:S(2)}) async-start(bf16[16,2,1,1024,256]{4,3,1,2,0:T(8,128)(2,1)} %bitcast.41), calls=%async_computation | async-start | bytes 33554432 | tf_op jit(solution)/shard_map/all_to_all | solution.py:43
  25.2 301.7 %reduce-scatter.2.cloned.1.call-start = ((), (), s32[]{:S(2)}) async-start(), calls=%async_computation.2 | async-start | bytes 294912 | tf_op jit(solution)/shard_map/reduce_scatter | solution.py:69
  274.1 10.5 %copy-start.2 = (bf16[16,1,256]{2,0,1:T(8,128)(2,1)S(1)}, bf16[16,1,256]{2,0,1:T(8,128)(2,1)}, u32[]{:S(2)}) copy-start(bf16[16,1,256]{2,0,1:T(8,128)(2,1)} %param.7) | copy-start | bytes 24580
Sparse Core Ops, SparseCore 0:
  299.1 27.8 reduce-scatter.1
where the time goes:
time: 338 us; the launch traced here: 335 us
  waiting for transfers between devices  276 us (82%)
  local copies, waits for them, and re-layouts  20.9 us (6%)
  between operations  13.5 us (4%)
  other arithmetic  9.94 us (3%)
  starting transfers between devices  7.74 us (2%)
  matrix products  7.27 us (2%)
    all_to_all x1, waiting for transfers between devices, shards(): lax.all_to_all(outgoing, 'rep', split_axis=0, concat_axis=0, tiled=True)  248 us
    reduce_scatter x1, waiting for transfers between devices, shards(): lax.psum_scatter(partial_terms, 'tp', scatter_dimension=1, tiled=True)  28 us
    gather x1, local copies, waits for them, and re-layouts, shards(): arrived.reshape((rep_count * MOST,) + arrived.shape[2:])[own_slot]  10.5 us
    gather x1, local copies, waits for them, and re-layouts, shards(): outgoing = parent_cache[send_index]  9.33 us
    all_to_all x1, starting transfers between devices, shards(): lax.all_to_all(outgoing, 'rep', split_axis=0, concat_axis=0, tiled=True)  7.7 us
    select_n x1, other arithmetic, shards(): jnp.where(inherit_mask, inherited, jnp.where(fresh_mask, new_kv[:, :, Non...  6.8 us
  transfers between devices with their start and end apart: 2, of which 2 were waited for; matrix products, arithmetic and copies ran while one was open for 0% of the time, Pallas kernels for 0%

commit v1 on v0

v1 whole, which is shorter than its diff:
```python
import functools

import jax
import jax.numpy as jnp
from jax import lax
from jax.experimental import pallas as pl
from jax.experimental.pallas import tpu as pltpu
from jax.sharding import PartitionSpec as P

MOST = 2
ROWS = 16
LANES = 4


def pack_kernel(parents, child_count, place, child_parent, queries, new_kv, packets, pick, seen):
    packets[...] = jnp.zeros_like(packets)
    holders = packets.shape[0] // MOST
    for h in range(holders):
        seen[h] = 0
    head_size = queries.shape[-1]
    base = place[0] * child_count
    row = lax.broadcasted_iota(jnp.int32, (8, head_size), 0)
    pick_row = lax.broadcasted_iota(jnp.int32, pick.shape, 0)
    pick_col = lax.broadcasted_iota(jnp.int32, pick.shape, 1) % (holders * MOST)
    chosen = jnp.zeros(pick.shape, jnp.bool_)
    for c in range(child_count):
        holder = lax.div(child_parent[base + c], parents)
        rank = seen[holder]
        seen[holder] = rank + 1
        slot = holder * MOST + rank
        fresh = new_kv[c].astype(jnp.float32)
        tail = jnp.where(row == 0, fresh[:, :head_size], fresh[:, head_size:])
        packet = jnp.concatenate([queries[c].astype(jnp.float32), tail], axis=0)
        packets[slot] = packet.astype(packets.dtype)
        chosen = chosen | ((pick_row == c) & (pick_col == slot))
    pick[...] = jnp.where(chosen, 1.0, 0.0).astype(pick.dtype)


def attend_kernel(
    parents, child_count, place, child_parent, parent_len, packets, cache_hbm, weight_hbm, out,
    cache, weight, heads, found, cache_sem, weight_sem,
):
    get_cache = pltpu.make_async_copy(cache_hbm, cache, cache_sem)
    get_weight = pltpu.make_async_copy(weight_hbm, weight, weight_sem)
    get_cache.start()
    get_weight.start()
    slots = packets.shape[0]
    reps = slots // MOST
    group, head_size = 8, packets.shape[-1]
    cache_len = cache.shape[1]
    me = place[0]
    heads[...] = jnp.zeros_like(heads)

    for i in range(slots + LANES):
        found[i] = slots * parents
    count = jnp.int32(0)
    for r in range(reps):
        rank = jnp.int32(0)
        for c in range(child_count):
            local = child_parent[r * child_count + c] - me * parents
            found[count] = (r * MOST + rank) * parents + local
            hit = ((local >= 0) & (local < parents)).astype(jnp.int32)
            count = count + hit
            rank = rank + hit
    for i in range(LANES):
        found[count + i] = slots * parents
    get_cache.wait()
    column = lax.broadcasted_iota(jnp.int32, (group, cache_len), 1)

    def some(step, carry):
        for lane in range(LANES):
            entry = found[step * LANES + lane]
            slot, local = lax.div(entry, parents), lax.rem(entry, parents)
            length = parent_len[me * parents + local]
            packet = packets[jnp.minimum(slot, slots - 1)]
            keys = cache[local, :, :head_size]
            values = cache[local, :, head_size:]
            scores = lax.dot_general(
                packet, keys, (((1,), (1,)), ((), ())), preferred_element_type=jnp.float32
            )[:group] * head_size ** (-0.5)
            wide = packet.astype(jnp.float32)
            query, new_key, new_value = wide[:group], wide[group : group + 1], wide[group + 1 : group + 2]
            new_score = jnp.sum(query * new_key, axis=1, keepdims=True) * head_size ** (-0.5)
            scores = jnp.where(column < length, scores, -jnp.inf)
            top = jnp.maximum(jnp.max(scores, axis=1, keepdims=True), new_score)
            weights = jnp.exp(scores - top)
            new_weight = jnp.exp(new_score - top)
            total = jnp.sum(weights, axis=1, keepdims=True) + new_weight
            summed = jnp.dot(
                weights.astype(jnp.bfloat16), values, preferred_element_type=jnp.float32
            )
            summed = summed + new_weight.astype(jnp.bfloat16).astype(jnp.float32) * new_value
            heads[pl.ds(pl.multiple_of(slot * group, group), group), :] = summed / total
        return carry

    lax.fori_loop(0, lax.div(count + LANES - 1, LANES), some, 0)
    left = jnp.concatenate(
        [heads[pl.ds(i, slots, stride=group), :].astype(jnp.bfloat16) for i in range(group)], axis=1
    )
    get_weight.wait()
    part = out.shape[1]
    for i in range(out.shape[0] // slots):
        out[i * slots : (i + 1) * slots, :] = jnp.dot(
            left, weight[:, i * part : (i + 1) * part], preferred_element_type=jnp.float32
        ).astype(out.dtype)


def shards(queries, new_kv, parent_cache, parent_len, child_parent, out_weight):
    reps = lax.axis_size("rep")
    tps = lax.axis_size("tp")
    parents, _, cache_len, width = parent_cache.shape
    child_count, group, head_size = queries.shape
    features = out_weight.shape[1]
    slots = reps * MOST
    place = lax.axis_index("rep").astype(jnp.int32).reshape(1)
    smem = pl.BlockSpec(memory_space=pltpu.SMEM)
    vmem = pl.BlockSpec(memory_space=pltpu.VMEM)
    anywhere = pl.BlockSpec(memory_space=pl.ANY)

    packets, pick = pl.pallas_call(
        functools.partial(pack_kernel, parents, child_count),
        out_shape=(
            jax.ShapeDtypeStruct((slots, ROWS, head_size), jnp.bfloat16),
            jax.ShapeDtypeStruct((child_count, tps * slots), jnp.bfloat16),
        ),
        in_specs=[smem, smem, vmem, vmem],
        out_specs=(vmem, vmem),
        scratch_shapes=[pltpu.SMEM((reps,), jnp.int32)],
    )(place, child_parent, queries, new_kv)
    packets = lax.all_to_all(packets, "rep", split_axis=0, concat_axis=0, tiled=True)

    partial = pl.pallas_call(
        functools.partial(attend_kernel, parents, child_count),
        out_shape=jax.ShapeDtypeStruct((tps * slots, features // tps), jnp.bfloat16),
        in_specs=[smem, smem, smem, vmem, anywhere, anywhere],
        out_specs=vmem,
        scratch_shapes=[
            pltpu.VMEM((parents, cache_len, width), jnp.bfloat16),
            pltpu.VMEM(out_weight.shape, jnp.bfloat16),
            pltpu.VMEM(((slots + 1) * group, head_size), jnp.float32),
            pltpu.SMEM((slots + 2 * LANES,), jnp.int32),
            pltpu.SemaphoreType.DMA,
            pltpu.SemaphoreType.DMA,
        ],
        compiler_params=pltpu.CompilerParams(vmem_limit_bytes=24 * 1024 * 1024),
    )(place, child_parent, parent_len, packets, parent_cache.reshape(parents, cache_len, width), out_weight)

    arrived = lax.all_to_all(partial, ("tp", "rep"), split_axis=0, concat_axis=0, tiled=True)
    return jnp.dot(pick, arrived, preferred_element_type=jnp.float32).astype(jnp.bfloat16)


def solution(mesh):
    placed = (
        P("rep", "tp", None),
        P("rep", "tp", None),
        P("rep", "tp", None, None),
        P(),
        P(),
        P("tp", None),
    )
    return jax.shard_map(
        shards, mesh=mesh, in_specs=placed, out_specs=P("rep", "tp"), check_vma=False
    )
```

time: 338 us -> 56.1 us (0.17)
  waiting for transfers between devices: 276 us -> 0 us
  blocking collectives: 0 us -> 34.9 us
  between operations: 13.5 us -> 0.03 us
  local copies, waits for them, and re-layouts: 20.9 us -> 8.43 us
  Pallas kernels: 0 us -> 11.8 us
  other arithmetic: 9.94 us -> 0 us
  starting transfers between devices: 7.74 us -> 0 us
  matrix products: 7.27 us -> 0.76 us
    all_to_all x1 -> x0, waiting for transfers between devices: 248 us -> none  [shards(): lax.all_to_all(outgoing, 'rep', split_axis=0, concat_axis=0, tiled=True)]
    all_to_all x0 -> x2, blocking collectives: none -> 34.9 us  [the longest x1 20.3 us: shards(): lax.all_to_all(partial, ('tp', 'rep'), split_axis=0, concat_axis=0, tiled...]
    reduce_scatter x1 -> x0, waiting for transfers between devices: 28 us -> none  [shards(): lax.psum_scatter(partial_terms, 'tp', scatter_dimension=1, tiled=True)]
    gather x3 -> x0, local copies, waits for them, and re-layouts: 20.5 us -> none  [the longest x1 10.5 us: shards(): arrived.reshape((rep_count * MOST,) + arrived.shape[2:])[own_slot]]
    pallas_call x0 -> x2, Pallas kernels: none -> 11.8 us  [the longest x1 10.3 us: shards(): pl.pallas_call(functools.partial(attend_kernel, parents, child_count), ou...]
    unnamed x8 -> x11, local copies, waits for them, and re-layouts: 0.02 us -> 8.22 us
    all_to_all x1 -> x0, starting transfers between devices: 7.7 us -> none  [shards(): lax.all_to_all(outgoing, 'rep', split_axis=0, concat_axis=0, tiled=True)]
    select_n x5 -> x0, other arithmetic: 7.59 us -> none  [the longest x1 6.8 us: shards(): jnp.where(inherit_mask, inherited, jnp.where(fresh_mask, new_kv[:, :, Non...]
  transfers between devices with their start and end apart: 2 -> 0, of which waited for: 2 -> 0; matrix products, arithmetic and copies ran while one was open for 0% -> 0% of each run, Pallas kernels for 0% -> 0%
where the time goes in v1:
time: 56.1 us; the launch traced here: 55.9 us
  blocking collectives  34.9 us (62%)
  Pallas kernels  11.8 us (21%)
  local copies, waits for them, and re-layouts  8.43 us (15%)
  matrix products  0.76 us (1%)
    all_to_all x1, blocking collectives, shards(): lax.all_to_all(partial, ('tp', 'rep'), split_axis=0, concat_axis=0, tiled...  20.3 us
    all_to_all x1, blocking collectives, shards(): lax.all_to_all(packets, 'rep', split_axis=0, concat_axis=0, tiled=True)  14.6 us
    pallas_call x1, Pallas kernels, shards(): pl.pallas_call(functools.partial(attend_kernel, parents, child_count), ou...  10.3 us
    unnamed x11, local copies, waits for them, and re-layouts  8.22 us
    pallas_call x1, Pallas kernels, shards(): pl.pallas_call(functools.partial(pack_kernel, parents, child_count), out_...  1.5 us

profile of v1, /device:TPU:1, one launch (start us, length us, event | category | flops | bytes accessed | tf_op | source)
XLA Modules:
  0.0 55.9 jit_solution(13161771665093204295)
XLA Ops:
  0.0 1.3 %copy.7.new_kv = bf16[16,1,256]{2,1,0:T(2,128)(2,1)} copy(bf16[16,1,256]{2,0,1:T(8,128)(2,1)} %param.7) | data formatting | bytes 16384 | tf_op args[1]
  1.3 1.5 %shard_map.64 = (bf16[32,16,128]{2,1,0:T(8,128)(2,1)}, bf16[16,256]{1,0:T(8,128)(2,1)}) custom-call(s32[1]{0:T(128)} %bitcast.place, s32[256]{0:T(256)} %child_parent.3, bf16[16,8,128]{2,1,0:T(8,128)(2,1)} %queries.1, bf16[16,1,256]{2,1,0:T(2,128)(2,1)} %copy.7.new_kv), custom_call_target="tpu_custom_call" | custom-call | tf_op jit(solution)/shard_map/pallas_call | solution.py:120
  2.8 0.0 copy-start.4
  2.8 14.6 %all_to_all.17.packets = bf16[32,16,128]{2,1,0:T(8,128)(2,1)S(1)} all-to-all(bf16[32,16,128]{2,1,0:T(8,128)(2,1)} %get-tuple-element.8), channel_id=1, replica_groups=mesh['rep'=16,'tp'=8] {'rep'}, dimensions={0} | all-to-all | bytes 262144 | tf_op jit(solution)/shard_map/all_to_all | solution.py:130
  17.4 0.0 copy-start
  17.4 3.4 %copy-done = bf16[1024,4096]{1,0:T(8,128)(2,1)S(1)} copy-done((bf16[1024,4096]{1,0:T(8,128)(2,1)S(1)}, bf16[1024,4096]{1,0:T(8,128)(2,1)}, u32[]{:S(2)}) %copy-start) | copy-done | bytes 8388632
  20.8 0.0 copy-start.1
  20.8 2.2 %copy-done.1 = bf16[8,1,1024,256]{3,2,1,0:T(8,128)(2,1)S(1)} copy-done((bf16[8,1,1024,256]{3,2,1,0:T(8,128)(2,1)S(1)}, bf16[8,1,1024,256]{3,2,1,0:T(8,128)(2,1)}, u32[]{:S(2)}) %copy-start.1) | copy-done | bytes 4194328
  23.0 0.0 copy-start.2
  23.0 0.7 %copy-done.2 = s32[256]{0:T(256)S(1)} copy-done((s32[256]{0:T(256)S(1)}, s32[256]{0:T(256)}, u32[]{:S(2)}) %copy-start.2) | copy-done | bytes 1048
  23.7 0.0 copy-start.3
  23.7 0.7 %copy-done.3 = s32[128]{0:T(128)S(1)} copy-done((s32[128]{0:T(128)S(1)}, s32[128]{0:T(128)}, u32[]{:S(2)}) %copy-start.3) | copy-done | bytes 536
  24.3 10.3 %shard_map.65 = bf16[256,512]{1,0:T(8,128)(2,1)S(1)} custom-call(s32[1]{0:T(128)} %bitcast.place, s32[256]{0:T(256)S(1)} %copy-done.2, s32[128]{0:T(128)S(1)} %copy-done.3, bf16[32,16,128]{2,1,0:T(8,128)(2,1)S(1)} %all_to_all.17.packets, bf16[8,1024,256]{2,1,0:T(8,128)(2,1)S(1)} %bitcast.4, bf16[1024,4096]{1,0:T(8,128)(2,1)S(1)} %copy-done), custom_call_target="tpu_custom_call" | custom-call | tf_op jit(solution)/shard_map/pallas_call | solution.py:132
  34.6 0.1 all_to_all.12
  34.8 20.3 %all_to_all.18 = bf16[128,2,512]{2,1,0:T(2,128)(2,1)S(1)} all-to-all(bf16[128,2,512]{2,1,0:T(2,128)(2,1)S(1)} %all_to_all.12), channel_id=1, replica_groups=mesh['rep'=16,'tp'=8] {'tp','rep'}, dimensions={0} | all-to-all | bytes 524288 | tf_op jit(solution)/shard_map/all_to_all | solution.py:148
  55.1 0.1 all_to_all.14
  55.2 0.0 copy-done.4
  55.2 0.8 %convolution_convert_fusion = bf16[16,512]{1,0:T(8,128)(2,1)} fusion(bf16[16,256]{1,0:T(8,128)(2,1)S(1)} %copy-done.4, bf16[256,512]{1,0:T(8,128)(2,1)S(1)} %all_to_all.14), kind=kOutput, calls=%fused_computation | convolution fusion | flops 4202496 | bytes 286720 | tf_op jit(solution)/shard_map/dot_general | solution.py:149
Async XLA Ops:
  2.8 52.4 %copy-start.4 = (bf16[16,256]{1,0:T(8,128)(2,1)S(1)}, bf16[16,256]{1,0:T(8,128)(2,1)}, u32[]{:S(2)}) copy-start(bf16[16,256]{1,0:T(8,128)(2,1)} %get-tuple-element.7) | copy-start | bytes 24580
  17.4 3.4 %copy-start = (bf16[1024,4096]{1,0:T(8,128)(2,1)S(1)}, bf16[1024,4096]{1,0:T(8,128)(2,1)}, u32[]{:S(2)}) copy-start(bf16[1024,4096]{1,0:T(8,128)(2,1)} %weight_hbm.1) | copy-start | bytes 25165828
  20.8 2.2 %copy-start.1 = (bf16[8,1,1024,256]{3,2,1,0:T(8,128)(2,1)S(1)}, bf16[8,1,1024,256]{3,2,1,0:T(8,128)(2,1)}, u32[]{:S(2)}) copy-start(bf16[8,1,1024,256]{3,2,1,0:T(8,128)(2,1)} %param.8) | copy-start | bytes 12582916
  23.0 0.7 %copy-start.2 = (s32[256]{0:T(256)S(1)}, s32[256]{0:T(256)}, u32[]{:S(2)}) copy-start(s32[256]{0:T(256)} %child_parent.3) | copy-start | bytes 3076
  23.7 0.7 %copy-start.3 = (s32[128]{0:T(128)S(1)}, s32[128]{0:T(128)}, u32[]{:S(2)}) copy-start(s32[128]{0:T(128)} %parent_len.1) | copy-start | bytes 1540

commit v2 on v1

v2 whole, which is shorter than its diff:
```python
import functools

import jax
import jax.numpy as jnp
from jax import lax
from jax.experimental import pallas as pl
from jax.experimental.pallas import tpu as pltpu
from jax.sharding import PartitionSpec as P

MOST = 2
ROWS = 16
GROUP = 8
LENGTHS, COUNTS, EXTRAS, EXTRA_COUNT, PLAN = 64, 72, 80, 127, 128
MIB = 1024 * 1024
NEAR = 6
TOGETHER = 4
WAVES = (0, 2), (2, 5), (5, 8)


def pack_kernel(parents, child_count, place, child_parent, queries, new_kv, packets, pick, seen):
    packets[...] = jnp.zeros_like(packets)
    holders = packets.shape[0] // MOST
    for h in range(holders):
        seen[h] = 0
    head_size = queries.shape[-1]
    base = place[0] * child_count
    row = lax.broadcasted_iota(jnp.int32, (8, head_size), 0)
    pick_row = lax.broadcasted_iota(jnp.int32, pick.shape, 0)
    pick_col = lax.broadcasted_iota(jnp.int32, pick.shape, 1) % (holders * MOST)
    chosen = jnp.zeros(pick.shape, jnp.bool_)
    for c in range(child_count):
        holder = lax.div(child_parent[base + c], parents)
        rank = seen[holder]
        seen[holder] = rank + 1
        slot = holder * MOST + rank
        fresh = new_kv[c : c + 1, :].astype(jnp.float32)
        tail = jnp.where(row == 0, fresh[:, :head_size], fresh[:, head_size:])
        packet = jnp.concatenate([queries[c].astype(jnp.float32), tail], axis=0)
        packets[slot] = packet.astype(packets.dtype)
        chosen = chosen | ((pick_row == c) & (pick_col == slot))
    pick[...] = jnp.where(chosen, 1.0, 0.0).astype(pick.dtype)


def ahead_kernel(
    parents, child_count, slots, place, child_parent, parent_len, cache_hbm, near, plan, hits, near_sem
):
    get_near = pltpu.make_async_copy(cache_hbm.at[pl.ds(0, near.shape[0])], near, near_sem)
    get_near.start()
    base = place[0] * parents
    for i in range(parents * GROUP):
        plan[i] = slots
    for p in range(parents):
        plan[LENGTHS + p] = parent_len[base + p]
        plan[COUNTS + p] = 0
    count = jnp.int32(0)
    for r in range(slots // MOST):
        rank = jnp.int32(0)
        for c in range(child_count):
            local = child_parent[r * child_count + c] - base
            hits[count] = (r * MOST + rank) * parents + local
            hit = ((local >= 0) & (local < parents)).astype(jnp.int32)
            count = count + hit
            rank = rank + hit

    def sort(i, extra):
        slot, local = lax.div(hits[i], parents), lax.rem(hits[i], parents)
        before = plan[COUNTS + local]
        plan[COUNTS + local] = before + 1
        fits = before < GROUP

        @pl.when(fits)
        def _():
            plan[local * GROUP + before] = slot

        @pl.when(jnp.logical_not(fits))
        def _():
            plan[EXTRAS + extra] = hits[i]

        return extra + jnp.where(fits, 0, 1)

    plan[EXTRA_COUNT] = lax.fori_loop(0, count, sort, jnp.int32(0))
    get_near.wait()


def attend(packet_lists, keys, values, lengths, group):
    head_size = keys[0].shape[1]
    scale = head_size ** (-0.5)
    wide = [[x.astype(jnp.float32) for x in packets] for packets in packet_lists]
    query = [jnp.concatenate([w[:group] for w in ws], axis=0) for ws in wide]
    scores = [
        lax.dot_general(q.astype(jnp.bfloat16), k, (((1,), (1,)), ((), ())), preferred_element_type=jnp.float32)
        for q, k in zip(query, keys)
    ]
    new_key = [jnp.concatenate([jnp.broadcast_to(w[group : group + 1], (group, head_size)) for w in ws], axis=0) for ws in wide]
    new_score = [jnp.sum(q * k, axis=1, keepdims=True) for q, k in zip(query, new_key)]
    column = lax.broadcasted_iota(jnp.int32, scores[0].shape, 1)
    scores = [jnp.where(column < n, s, -jnp.inf) for s, n in zip(scores, lengths)]
    top = [jnp.maximum(jnp.max(s, axis=1, keepdims=True), x) for s, x in zip(scores, new_score)]
    weights = [jnp.exp((s - t) * scale) for s, t in zip(scores, top)]
    summed = [
        jnp.dot(w.astype(jnp.bfloat16), v, preferred_element_type=jnp.float32) for w, v in zip(weights, values)
    ]
    new_weight = [jnp.exp((x - t) * scale) for x, t in zip(new_score, top)]
    total = [jnp.sum(w, axis=1, keepdims=True) + x for w, x in zip(weights, new_weight)]
    new_value = [jnp.concatenate([jnp.broadcast_to(w[group + 1 : group + 2], (group, head_size)) for w in ws], axis=0) for ws in wide]
    return [
        (s + x.astype(jnp.bfloat16).astype(jnp.float32) * v) / t
        for s, x, v, t in zip(summed, new_weight, new_value, total)
    ]


def attend_kernel(
    parents, plan_in, packets, near, cache_hbm, weight_hbm, out,
    plan, far, weight, heads, plan_sem, far_sem, weight_sems,
):
    slots = packets.shape[0]
    group, head_size = 8, packets.shape[-1]
    part = out.shape[1]
    parts = out.shape[0] // slots
    near_count = near.shape[0]
    get_far = pltpu.make_async_copy(cache_hbm.at[pl.ds(near_count, parents - near_count)], far, far_sem)
    get_weight = [
        pltpu.make_async_copy(
            weight_hbm.at[:, pl.ds(i * part, part)], weight.at[:, pl.ds(i * part, part)], weight_sems.at[i]
        )
        for i in range(parts)
    ]
    get_plan = pltpu.make_async_copy(plan_in, plan, plan_sem)
    get_plan.start()
    get_far.start()
    for i in range(*WAVES[0]):
        get_weight[i].start()
    get_plan.wait()
    heads[...] = jnp.zeros_like(heads)

    def block(p):
        return (near, p) if p < near_count else (far, p - near_count)

    for first in range(0, parents, TOGETHER):
        if first + TOGETHER > near_count:
            get_far.wait()
        some = range(first, first + TOGETHER)
        places = [[plan[p * GROUP + k] for k in range(GROUP)] for p in some]
        results = attend(
            [[packets[jnp.minimum(at, slots - 1)] for at in spots] for spots in places],
            [block(p)[0][block(p)[1], :, :head_size] for p in some],
            [block(p)[0][block(p)[1], :, head_size:] for p in some],
            [plan[LENGTHS + p] for p in some],
            group,
        )
        for spots, result in zip(places, results):
            for k, at in enumerate(spots):
                heads[pl.ds(pl.multiple_of(at * group, group), group), :] = result[k * group : (k + 1) * group]
        if first == 0:
            for i in range(*WAVES[1]):
                get_weight[i].start()

    for i in range(*WAVES[2]):
        get_weight[i].start()

    def one(keys, at, local):
        return attend([[packets[at]]], [keys[:, :head_size]], [keys[:, head_size:]], [plan[LENGTHS + local]], group)[0]

    def extra(i, carry):
        at, local = lax.div(plan[EXTRAS + i], parents), lax.rem(plan[EXTRAS + i], parents)
        rows = pl.ds(pl.multiple_of(at * group, group), group)

        @pl.when(local < near_count)
        def _():
            heads[rows, :] = one(near[jnp.minimum(local, near_count - 1)], at, local)

        @pl.when(local >= near_count)
        def _():
            heads[rows, :] = one(far[jnp.maximum(local - near_count, 0)], at, local)

        return carry

    lax.fori_loop(0, plan[EXTRA_COUNT], extra, 0)
    left = jnp.concatenate(
        [heads[pl.ds(i, slots, stride=group), :].astype(jnp.bfloat16) for i in range(group)], axis=1
    )
    for i in range(parts):
        get_weight[i].wait()
        out[i * slots : (i + 1) * slots, :] = jnp.dot(
            left, weight[:, i * part : (i + 1) * part], preferred_element_type=jnp.float32
        ).astype(out.dtype)


def shards(queries, new_kv, parent_cache, parent_len, child_parent, out_weight):
    reps = lax.axis_size("rep")
    tps = lax.axis_size("tp")
    parents, _, cache_len, width = parent_cache.shape
    child_count, group, head_size = queries.shape
    features = out_weight.shape[1]
    slots = reps * MOST
    place = lax.axis_index("rep").astype(jnp.int32).reshape(1)
    smem = pl.BlockSpec(memory_space=pltpu.SMEM)
    vmem = pl.BlockSpec(memory_space=pltpu.VMEM)
    anywhere = pl.BlockSpec(memory_space=pl.ANY)

    packets, pick = pl.pallas_call(
        functools.partial(pack_kernel, parents, child_count),
        out_shape=(
            jax.ShapeDtypeStruct((slots, ROWS, head_size), jnp.bfloat16),
            jax.ShapeDtypeStruct((child_count, tps * slots), jnp.bfloat16),
        ),
        in_specs=[smem, smem, vmem, vmem],
        out_specs=(vmem, vmem),
        scratch_shapes=[pltpu.SMEM((reps,), jnp.int32)],
    )(place, child_parent, queries, new_kv.reshape(child_count, width))
    packets = lax.all_to_all(packets, "rep", split_axis=0, concat_axis=0, tiled=True)

    caches = parent_cache.reshape(parents, cache_len, width)
    near, plan = pl.pallas_call(
        functools.partial(ahead_kernel, parents, child_count, slots),
        out_shape=(
            jax.ShapeDtypeStruct((NEAR, cache_len, width), caches.dtype),
            jax.ShapeDtypeStruct((PLAN,), jnp.int32),
        ),
        in_specs=[smem, smem, smem, anywhere],
        out_specs=(vmem, smem),
        scratch_shapes=[pltpu.SMEM((slots + 1,), jnp.int32), pltpu.SemaphoreType.DMA],
        compiler_params=pltpu.CompilerParams(vmem_limit_bytes=50 * MIB),
        cost_estimate=pl.CostEstimate(flops=0, bytes_accessed=8 * MIB, transcendentals=0),
    )(place, child_parent, parent_len, caches)

    partial = pl.pallas_call(
        functools.partial(attend_kernel, parents),
        out_shape=jax.ShapeDtypeStruct((tps * slots, features // tps), jnp.bfloat16),
        in_specs=[anywhere, vmem, vmem, anywhere, anywhere],
        out_specs=vmem,
        scratch_shapes=[
            pltpu.SMEM((PLAN,), jnp.int32),
            pltpu.VMEM((parents - NEAR, cache_len, width), jnp.bfloat16),
            pltpu.VMEM(out_weight.shape, jnp.bfloat16),
            pltpu.VMEM(((slots + 1) * group, head_size), jnp.float32),
            pltpu.SemaphoreType.DMA,
            pltpu.SemaphoreType.DMA,
            pltpu.SemaphoreType.DMA((tps,)),
        ],
        compiler_params=pltpu.CompilerParams(vmem_limit_bytes=50 * MIB),
    )(plan, packets, near, caches, out_weight)

    arrived = lax.all_to_all(partial, ("tp", "rep"), split_axis=0, concat_axis=0, tiled=True)
    return jnp.dot(pick, arrived, preferred_element_type=jnp.float32).astype(jnp.bfloat16)


def solution(mesh):
    placed = (
        P("rep", "tp", None),
        P("rep", "tp", None),
        P("rep", "tp", None, None),
        P(),
        P(),
        P("tp", None),
    )
    return jax.shard_map(
        shards, mesh=mesh, in_specs=placed, out_specs=P("rep", "tp"), check_vma=False
    )
```

time: 56.1 us -> 41.9 us (0.75)
  blocking collectives: 34.9 us -> 19.7 us
  starting transfers between devices: 0 us -> 7.58 us
  local copies, waits for them, and re-layouts: 8.43 us -> 1.54 us
  waiting for transfers between devices: 0 us -> 2.48 us
  Pallas kernels: 11.8 us -> 9.38 us
    all_to_all x1 -> x0, blocking collectives: 14.6 us -> none  [shards(): lax.all_to_all(packets, 'rep', split_axis=0, concat_axis=0, tiled=True)]
    all_to_all x0 -> x1, starting transfers between devices: none -> 7.58 us  [shards(): lax.all_to_all(packets, 'rep', split_axis=0, concat_axis=0, tiled=True)]
    unnamed x11 -> x6, local copies, waits for them, and re-layouts: 8.22 us -> 1.33 us
    all_to_all x0 -> x1, waiting for transfers between devices: none -> 2.48 us  [shards(): lax.all_to_all(packets, 'rep', split_axis=0, concat_axis=0, tiled=True)]
    pallas_call x1 -> x2, Pallas kernels: 10.3 us -> 7.88 us  [the longest x1 4.84 us: shards(): pl.pallas_call(functools.partial(attend_kernel, parents), out_shape=jax.S...]
    all_to_all x1, blocking collectives: 20.3 us -> 19.7 us  [shards(): lax.all_to_all(partial, ('tp', 'rep'), split_axis=0, concat_axis=0, tiled...]
  transfers between devices with their start and end apart: 0 -> 1, of which waited for: 0 -> 1; matrix products, arithmetic and copies ran while one was open for 0% -> 0% of each run, Pallas kernels for 0% -> 7%
where the time goes in v2:
time: 41.9 us; the launch traced here: 41.5 us
  blocking collectives  19.7 us (47%)
  Pallas kernels  9.38 us (22%)
  starting transfers between devices  7.58 us (18%)
  waiting for transfers between devices  2.48 us (6%)
  local copies, waits for them, and re-layouts  1.54 us (4%)
  matrix products  0.76 us (2%)
    all_to_all x1, blocking collectives, shards(): lax.all_to_all(partial, ('tp', 'rep'), split_axis=0, concat_axis=0, tiled...  19.7 us
    all_to_all x1, starting transfers between devices, shards(): lax.all_to_all(packets, 'rep', split_axis=0, concat_axis=0, tiled=True)  7.58 us
    pallas_call x1, Pallas kernels, shards(): pl.pallas_call(functools.partial(attend_kernel, parents), out_shape=jax.S...  4.84 us
    pallas_call x1, Pallas kernels, shards(): pl.pallas_call(functools.partial(ahead_kernel, parents, child_count, slot...  3.04 us
    all_to_all x1, waiting for transfers between devices, shards(): lax.all_to_all(packets, 'rep', split_axis=0, concat_axis=0, tiled=True)  2.48 us
    pallas_call x1, Pallas kernels, shards(): pl.pallas_call(functools.partial(pack_kernel, parents, child_count), out_...  1.5 us
    unnamed x6, local copies, waits for them, and re-layouts  1.33 us
  transfers between devices with their start and end apart: 1, of which 1 were waited for; matrix products, arithmetic and copies ran while one was open for 0% of the time, Pallas kernels for 7%

profile of v2, /device:TPU:1, one launch (start us, length us, event | category | flops | bytes accessed | tf_op | source)
XLA Modules:
  0.0 41.5 jit_solution(7399738340923328177)
XLA Ops:
  0.0 1.5 %shard_map.64 = (bf16[32,16,128]{2,1,0:T(8,128)(2,1)}, bf16[16,256]{1,0:T(8,128)(2,1)}) custom-call(s32[1]{0:T(128)} %bitcast.place, s32[256]{0:T(256)} %child_parent.3, bf16[16,8,128]{2,1,0:T(8,128)(2,1)} %queries.1, bf16[16,256]{1,0:T(8,128)(2,1)} %bitcast.7), custom_call_target="tpu_custom_call" | custom-call | tf_op jit(solution)/shard_map/pallas_call | solution.py:201
  1.5 7.6 %all-to-all-start = ((bf16[32,16,128]{2,1,0:T(8,128)(2,1)}), bf16[32,16,128]{2,1,0:T(8,128)(2,1)S(1)}, u32[]{:S(2)}, u32[]{:S(2)}) async-start(bf16[32,16,128]{2,1,0:T(8,128)(2,1)} %get-tuple-element.11), calls=%async_computation | async-start | bytes 262144 | tf_op jit(solution)/shard_map/all_to_all | solution.py:211
  9.1 0.0 copy-start
  9.1 0.7 %copy-done = s32[256]{0:T(256)S(1)} copy-done((s32[256]{0:T(256)S(1)}, s32[256]{0:T(256)}, u32[]{:S(2)}) %copy-start) | copy-done | bytes 1048
  9.8 0.0 copy-start.1
  9.8 0.7 %copy-done.1 = s32[128]{0:T(128)S(1)} copy-done((s32[128]{0:T(128)S(1)}, s32[128]{0:T(128)}, u32[]{:S(2)}) %copy-start.1) | copy-done | bytes 536
  10.4 3.0 %shard_map.65 = (bf16[6,1024,256]{2,1,0:T(8,128)(2,1)S(1)}, s32[128]{0:T(128)S(1)}) custom-call(s32[1]{0:T(128)} %bitcast.place, s32[256]{0:T(256)S(1)} %copy-done, s32[128]{0:T(128)S(1)} %copy-done.1, bf16[8,1024,256]{2,1,0:T(8,128)(2,1)} %bitcast.5), custom_call_target="tpu_custom_call" | custom-call | bytes 8388608 | tf_op jit(solution)/shard_map/pallas_call | solution.py:214
  13.5 2.5 %all-to-all-done.packets = bf16[32,16,128]{2,1,0:T(8,128)(2,1)S(1)} async-done(((bf16[32,16,128]{2,1,0:T(8,128)(2,1)}), bf16[32,16,128]{2,1,0:T(8,128)(2,1)S(1)}, u32[]{:S(2)}, u32[]{:S(2)}) %all-to-all-start) | async-done | bytes 131104 | tf_op jit(solution)/shard_map/all_to_all | solution.py:211
  16.0 0.0 copy-start.2
  16.0 4.8 %shard_map.66 = bf16[256,512]{1,0:T(8,128)(2,1)S(1)} custom-call(s32[128]{0:T(128)S(1)} %get-tuple-element.10.plan_in, bf16[32,16,128]{2,1,0:T(8,128)(2,1)S(1)} %all-to-all-done.packets, bf16[6,1024,256]{2,1,0:T(8,128)(2,1)S(1)} %get-tuple-element.12.near, bf16[8,1024,256]{2,1,0:T(8,128)(2,1)} %bitcast.6, bf16[1024,4096]{1,0:T(8,128)(2,1)} %weight_hbm.1), custom_call_target="tpu_custom_call" | custom-call | tf_op jit(solution)/shard_map/pallas_call | solution.py:227
  20.8 0.1 all_to_all.12
  20.9 19.7 %all_to_all.17 = bf16[128,2,512]{2,1,0:T(2,128)(2,1)S(1)} all-to-all(bf16[128,2,512]{2,1,0:T(2,128)(2,1)S(1)} %all_to_all.12), channel_id=1, replica_groups=mesh['rep'=16,'tp'=8] {'tp','rep'}, dimensions={0} | all-to-all | bytes 524288 | tf_op jit(solution)/shard_map/all_to_all | solution.py:244
  40.6 0.1 all_to_all.14
  40.8 0.0 copy-done.2
  40.8 0.8 %convolution_convert_fusion = bf16[16,512]{1,0:T(8,128)(2,1)} fusion(bf16[16,256]{1,0:T(8,128)(2,1)S(1)} %copy-done.2, bf16[256,512]{1,0:T(8,128)(2,1)S(1)} %all_to_all.14), kind=kOutput, calls=%fused_computation | convolution fusion | flops 4202496 | bytes 286720 | tf_op jit(solution)/shard_map/dot_general | solution.py:245
Async XLA Ops:
  1.5 14.5 %all-to-all-start = ((bf16[32,16,128]{2,1,0:T(8,128)(2,1)}), bf16[32,16,128]{2,1,0:T(8,128)(2,1)S(1)}, u32[]{:S(2)}, u32[]{:S(2)}) async-start(bf16[32,16,128]{2,1,0:T(8,128)(2,1)} %get-tuple-element.11), calls=%async_computation | async-start | bytes 262144 | tf_op jit(solution)/shard_map/all_to_all | solution.py:211
  9.1 0.7 %copy-start = (s32[256]{0:T(256)S(1)}, s32[256]{0:T(256)}, u32[]{:S(2)}) copy-start(s32[256]{0:T(256)} %child_parent.3) | copy-start | bytes 3076
  9.8 0.7 %copy-start.1 = (s32[128]{0:T(128)S(1)}, s32[128]{0:T(128)}, u32[]{:S(2)}) copy-start(s32[128]{0:T(128)} %parent_len.1) | copy-start | bytes 1540
  16.0 24.8 %copy-start.2 = (bf16[16,256]{1,0:T(8,128)(2,1)S(1)}, bf16[16,256]{1,0:T(8,128)(2,1)}, u32[]{:S(2)}) copy-start(bf16[16,256]{1,0:T(8,128)(2,1)} %get-tuple-element.9) | copy-start | bytes 24580

commit v3 on v2

--- a/solution.py
+++ b/solution.py
@@ -10,14 +10,16 @@
 MOST = 2
 ROWS = 16
 GROUP = 8
-LENGTHS, COUNTS, EXTRAS, EXTRA_COUNT, PLAN = 64, 72, 80, 127, 128
+COUNTS, EXTRAS, EXTRA_COUNT, PLAN = 64, 80, 127, 128
 MIB = 1024 * 1024
+LOG2_E = 1.4426950408889634
 NEAR = 6
-TOGETHER = 4
+STAGES = (0, 1, 2, 3), (4, 5, 6, 7)
 WAVES = (0, 2), (2, 5), (5, 8)
-
-
-def pack_kernel(parents, child_count, place, child_parent, queries, new_kv, packets, pick, seen):
+LATE = {}
+
+
+def pack_kernel(parents, child_count, place, child_parent, parent_len, queries, new_kv, packets, pick, seen):
     packets[...] = jnp.zeros_like(packets)
     holders = packets.shape[0] // MOST
     for h in range(holders):
@@ -29,12 +31,16 @@
     pick_col = lax.broadcasted_iota(jnp.int32, pick.shape, 1) % (holders * MOST)
     chosen = jnp.zeros(pick.shape, jnp.bool_)
     for c in range(child_count):
-        holder = lax.div(child_parent[base + c], parents)
+        parent = child_parent[base + c]
+        holder = lax.div(parent, parents)
         rank = seen[holder]
         seen[holder] = rank + 1
         slot = holder * MOST + rank
         fresh = new_kv[c : c + 1, :].astype(jnp.float32)
+        length = parent_len[parent]
+        high, low = lax.div(length, 32).astype(jnp.float32), lax.rem(length, 32).astype(jnp.float32)
         tail = jnp.where(row == 0, fresh[:, :head_size], fresh[:, head_size:])
+        tail = jnp.where(row < 2, tail, jnp.where(row == 2, high, low))
         packet = jnp.concatenate([queries[c].astype(jnp.float32), tail], axis=0)
         packets[slot] = packet.astype(packets.dtype)
         chosen = chosen | ((pick_row == c) & (pick_col == slot))
@@ -42,16 +48,19 @@
 
 
 def ahead_kernel(
-    parents, child_count, slots, place, child_parent, parent_len, cache_hbm, near, plan, hits, near_sem
+    parents, child_count, slots, place, child_parent_in, cache_hbm, near, plan,
+    child_parent, hits, near_sem, parent_sem,
 ):
     get_near = pltpu.make_async_copy(cache_hbm.at[pl.ds(0, near.shape[0])], near, near_sem)
+    get_parent = pltpu.make_async_copy(child_parent_in, child_parent, parent_sem)
+    get_parent.start()
     get_near.start()
     base = place[0] * parents
     for i in range(parents * GROUP):
         plan[i] = slots
     for p in range(parents):
-        plan[LENGTHS + p] = parent_len[base + p]
         plan[COUNTS + p] = 0
+    get_parent.wait()
     count = jnp.int32(0)
     for r in range(slots // MOST):
         rank = jnp.int32(0)
@@ -82,27 +91,32 @@
     get_near.wait()
 
 
-def attend(packet_lists, keys, values, lengths, group):
+def attend(packet_lists, keys, values, group):
     head_size = keys[0].shape[1]
-    scale = head_size ** (-0.5)
+    scale = head_size ** (-0.5) * LOG2_E
+
+    def row_of(packet, i):
+        return jnp.broadcast_to(packet[group + i : group + i + 1], (group, head_size))
+
     wide = [[x.astype(jnp.float32) for x in packets] for packets in packet_lists]
     query = [jnp.concatenate([w[:group] for w in ws], axis=0) for ws in wide]
     scores = [
         lax.dot_general(q.astype(jnp.bfloat16), k, (((1,), (1,)), ((), ())), preferred_element_type=jnp.float32)
         for q, k in zip(query, keys)
     ]
-    new_key = [jnp.concatenate([jnp.broadcast_to(w[group : group + 1], (group, head_size)) for w in ws], axis=0) for ws in wide]
+    new_key = [jnp.concatenate([row_of(w, 0) for w in ws], axis=0) for ws in wide]
     new_score = [jnp.sum(q * k, axis=1, keepdims=True) for q, k in zip(query, new_key)]
-    column = lax.broadcasted_iota(jnp.int32, scores[0].shape, 1)
-    scores = [jnp.where(column < n, s, -jnp.inf) for s, n in zip(scores, lengths)]
+    column = lax.broadcasted_iota(jnp.int32, (group, scores[0].shape[1]), 1).astype(jnp.float32)
+    bias = [jnp.where(column < row_of(ws[0], 2)[:, :1] * 32.0 + row_of(ws[0], 3)[:, :1], 0.0, -jnp.inf) for ws in wide]
+    scores = [s + jnp.concatenate([b] * len(ws), axis=0) for s, b, ws in zip(scores, bias, wide)]
     top = [jnp.maximum(jnp.max(s, axis=1, keepdims=True), x) for s, x in zip(scores, new_score)]
-    weights = [jnp.exp((s - t) * scale) for s, t in zip(scores, top)]
+    weights = [jnp.exp2((s - t) * scale) for s, t in zip(scores, top)]
     summed = [
         jnp.dot(w.astype(jnp.bfloat16), v, preferred_element_type=jnp.float32) for w, v in zip(weights, values)
     ]
-    new_weight = [jnp.exp((x - t) * scale) for x, t in zip(new_score, top)]
+    new_weight = [jnp.exp2((x - t) * scale) for x, t in zip(new_score, top)]
     total = [jnp.sum(w, axis=1, keepdims=True) + x for w, x in zip(weights, new_weight)]
-    new_value = [jnp.concatenate([jnp.broadcast_to(w[group + 1 : group + 2], (group, head_size)) for w in ws], axis=0) for ws in wide]
+    new_value = [jnp.concatenate([row_of(w, 1) for w in ws], axis=0) for ws in wide]
     return [
         (s + x.astype(jnp.bfloat16).astype(jnp.float32) * v) / t
         for s, x, v, t in zip(summed, new_weight, new_value, total)
@@ -136,30 +150,24 @@
     def block(p):
         return (near, p) if p < near_count else (far, p - near_count)
 
-    for first in range(0, parents, TOGETHER):
-        if first + TOGETHER > near_count:
+    for stage, some in enumerate(STAGES):
+        if some[-1] == parents - 1:
             get_far.wait()
-        some = range(first, first + TOGETHER)
         places = [[plan[p * GROUP + k] for k in range(GROUP)] for p in some]
         results = attend(
             [[packets[jnp.minimum(at, slots - 1)] for at in spots] for spots in places],
             [block(p)[0][block(p)[1], :, :head_size] for p in some],
             [block(p)[0][block(p)[1], :, head_size:] for p in some],
-            [plan[LENGTHS + p] for p in some],
             group,
         )
         for spots, result in zip(places, results):
             for k, at in enumerate(spots):
                 heads[pl.ds(pl.multiple_of(at * group, group), group), :] = result[k * group : (k + 1) * group]
-        if first == 0:
-            for i in range(*WAVES[1]):
-                get_weight[i].start()
-
-    for i in range(*WAVES[2]):
-        get_weight[i].start()
-
-    def one(keys, at, local):
-        return attend([[packets[at]]], [keys[:, :head_size]], [keys[:, head_size:]], [plan[LENGTHS + local]], group)[0]
+        for i in range(*WAVES[stage + 1]):
+            get_weight[i].start()
+
+    def one(keys, at):
+        return attend([[packets[at]]], [keys[:, :head_size]], [keys[:, head_size:]], group)[0]
 
     def extra(i, carry):
         at, local = lax.div(plan[EXTRAS + i], parents), lax.rem(plan[EXTRAS + i], parents)
@@ -167,11 +175,11 @@
 
         @pl.when(local < near_count)
         def _():
-            heads[rows, :] = one(near[jnp.minimum(local, near_count - 1)], at, local)
+            heads[rows, :] = one(near[jnp.minimum(local, near_count - 1)], at)
 
         @pl.when(local >= near_count)
         def _():
-            heads[rows, :] = one(far[jnp.maximum(local - near_count, 0)], at, local)
+            heads[rows, :] = one(far[jnp.maximum(local - near_count, 0)], at)
 
         return carry
 
@@ -181,6 +189,8 @@
     )
     for i in range(parts):
         get_weight[i].wait()
+        for j in range(*LATE.get(i, (0, 0))):
+            get_weight[j].start()
         out[i * slots : (i + 1) * slots, :] = jnp.dot(
             left, weight[:, i * part : (i + 1) * part], preferred_element_type=jnp.float32
         ).astype(out.dtype)
@@ -204,10 +214,10 @@
             jax.ShapeDtypeStruct((slots, ROWS, head_size), jnp.bfloat16),
             jax.ShapeDtypeStruct((child_count, tps * slots), jnp.bfloat16),
         ),
-        in_specs=[smem, smem, vmem, vmem],
+        in_specs=[smem, smem, smem, vmem, vmem],
         out_specs=(vmem, vmem),
         scratch_shapes=[pltpu.SMEM((reps,), jnp.int32)],
-    )(place, child_parent, queries, new_kv.reshape(child_count, width))
+    )(place, child_parent, parent_len, queries, new_kv.reshape(child_count, width))
     packets = lax.all_to_all(packets, "rep", split_axis=0, concat_axis=0, tiled=True)
 
     caches = parent_cache.reshape(parents, cache_len, width)
@@ -217,12 +227,17 @@
             jax.ShapeDtypeStruct((NEAR, cache_len, width), caches.dtype),
             jax.ShapeDtypeStruct((PLAN,), jnp.int32),
         ),
-        in_specs=[smem, smem, smem, anywhere],
+        in_specs=[smem, anywhere, anywhere],
         out_specs=(vmem, smem),
-        scratch_shapes=[pltpu.SMEM((slots + 1,), jnp.int32), pltpu.SemaphoreType.DMA],
+        scratch_shapes=[
+            pltpu.SMEM(child_parent.shape, jnp.int32),
+            pltpu.SMEM((slots + 1,), jnp.int32),
+            pltpu.SemaphoreType.DMA,
+            pltpu.SemaphoreType.DMA,
+        ],
         compiler_params=pltpu.CompilerParams(vmem_limit_bytes=50 * MIB),
         cost_estimate=pl.CostEstimate(flops=0, bytes_accessed=8 * MIB, transcendentals=0),
-    )(place, child_parent, parent_len, caches)
+    )(place, child_parent, caches)
 
     partial = pl.pallas_call(
         functools.partial(attend_kernel, parents),

time: 41.9 us -> 41.5 us (level)
  waiting for transfers between devices: 2.48 us -> 3.68 us
  local copies, waits for them, and re-layouts: 1.54 us -> 0.88 us
  Pallas kernels: 9.38 us -> 8.87 us
    all_to_all x1, waiting for transfers between devices: 2.48 us -> 3.68 us  [shards(): lax.all_to_all(packets, 'rep', split_axis=0, concat_axis=0, tiled=True)]
    unnamed x6 -> x4, local copies, waits for them, and re-layouts: 1.33 us -> 0.68 us
    pallas_call x1, Pallas kernels: 3.04 us -> 2.5 us  [shards(): pl.pallas_call(functools.partial(ahead_kernel, parents, child_count, slot...]
  transfers between devices with their start and end apart: 1 -> 1, of which waited for: 1 -> 1; matrix products, arithmetic and copies ran while one was open for 0% -> 0% of each run, Pallas kernels for 7% -> 6%
where the time goes in v3:
time: 41.5 us; the launch traced here: 41.2 us
  blocking collectives  19.4 us (47%)
  Pallas kernels  8.87 us (21%)
  starting transfers between devices  7.58 us (18%)
  waiting for transfers between devices  3.68 us (9%)
  local copies, waits for them, and re-layouts  0.88 us (2%)
  matrix products  0.76 us (2%)
    all_to_all x1, blocking collectives, shards(): lax.all_to_all(partial, ('tp', 'rep'), split_axis=0, concat_axis=0, tiled...  19.4 us
    all_to_all x1, starting transfers between devices, shards(): lax.all_to_all(packets, 'rep', split_axis=0, concat_axis=0, tiled=True)  7.58 us
    pallas_call x1, Pallas kernels, shards(): pl.pallas_call(functools.partial(attend_kernel, parents), out_shape=jax.S...  4.81 us
    all_to_all x1, waiting for transfers between devices, shards(): lax.all_to_all(packets, 'rep', split_axis=0, concat_axis=0, tiled=True)  3.68 us
    pallas_call x1, Pallas kernels, shards(): pl.pallas_call(functools.partial(ahead_kernel, parents, child_count, slot...  2.5 us
    pallas_call x1, Pallas kernels, shards(): pl.pallas_call(functools.partial(pack_kernel, parents, child_count), out_...  1.56 us
  transfers between devices with their start and end apart: 1, of which 1 were waited for; matrix products, arithmetic and copies ran while one was open for 0% of the time, Pallas kernels for 6%

profile of v3, /device:TPU:1, one launch (start us, length us, event | category | flops | bytes accessed | tf_op | source)
XLA Modules:
  0.0 41.2 jit_solution(5629324088676336363)
XLA Ops:
  0.0 1.6 %shard_map.64 = (bf16[32,16,128]{2,1,0:T(8,128)(2,1)}, bf16[16,256]{1,0:T(8,128)(2,1)}) custom-call(s32[1]{0:T(128)} %bitcast.place, s32[256]{0:T(256)} %child_parent_in.1, s32[128]{0:T(128)} %parent_len.1, bf16[16,8,128]{2,1,0:T(8,128)(2,1)} %queries.1, bf16[16,256]{1,0:T(8,128)(2,1)} %bitcast.7), custom_call_target="tpu_custom_call" | custom-call | tf_op jit(solution)/shard_map/pallas_call | solution.py:211
  1.6 7.6 %all-to-all-start = ((bf16[32,16,128]{2,1,0:T(8,128)(2,1)}), bf16[32,16,128]{2,1,0:T(8,128)(2,1)S(1)}, u32[]{:S(2)}, u32[]{:S(2)}) async-start(bf16[32,16,128]{2,1,0:T(8,128)(2,1)} %get-tuple-element.11), calls=%async_computation | async-start | bytes 262144 | tf_op jit(solution)/shard_map/all_to_all | solution.py:221
  9.2 0.0 copy-start
  9.2 0.7 %copy-done = s32[256]{0:T(256)S(1)} copy-done((s32[256]{0:T(256)S(1)}, s32[256]{0:T(256)}, u32[]{:S(2)}) %copy-start) | copy-done | bytes 1048
  9.8 2.5 %shard_map.65 = (bf16[6,1024,256]{2,1,0:T(8,128)(2,1)S(1)}, s32[128]{0:T(128)S(1)}) custom-call(s32[1]{0:T(128)} %bitcast.place, s32[256]{0:T(256)S(1)} %copy-done, bf16[8,1024,256]{2,1,0:T(8,128)(2,1)} %bitcast.5), custom_call_target="tpu_custom_call" | custom-call | bytes 8388608 | tf_op jit(solution)/shard_map/pallas_call | solution.py:224
  12.3 3.7 %all-to-all-done.packets = bf16[32,16,128]{2,1,0:T(8,128)(2,1)S(1)} async-done(((bf16[32,16,128]{2,1,0:T(8,128)(2,1)}), bf16[32,16,128]{2,1,0:T(8,128)(2,1)S(1)}, u32[]{:S(2)}, u32[]{:S(2)}) %all-to-all-start) | async-done | bytes 131104 | tf_op jit(solution)/shard_map/all_to_all | solution.py:221
  16.0 0.0 copy-start.1
  16.0 4.8 %shard_map.66 = bf16[256,512]{1,0:T(8,128)(2,1)S(1)} custom-call(s32[128]{0:T(128)S(1)} %get-tuple-element.10.plan_in, bf16[32,16,128]{2,1,0:T(8,128)(2,1)S(1)} %all-to-all-done.packets, bf16[6,1024,256]{2,1,0:T(8,128)(2,1)S(1)} %get-tuple-element.12.near, bf16[8,1024,256]{2,1,0:T(8,128)(2,1)} %bitcast.6, bf16[1024,4096]{1,0:T(8,128)(2,1)} %weight_hbm.1), custom_call_target="tpu_custom_call" | custom-call | tf_op jit(solution)/shard_map/pallas_call | solution.py:242
  20.8 0.1 all_to_all.12
  20.9 19.4 %all_to_all.17 = bf16[128,2,512]{2,1,0:T(2,128)(2,1)S(1)} all-to-all(bf16[128,2,512]{2,1,0:T(2,128)(2,1)S(1)} %all_to_all.12), channel_id=1, replica_groups=mesh['rep'=16,'tp'=8] {'tp','rep'}, dimensions={0} | all-to-all | bytes 524288 | tf_op jit(solution)/shard_map/all_to_all | solution.py:259
  40.3 0.1 all_to_all.14
  40.4 0.0 copy-done.1
  40.4 0.8 %convolution_convert_fusion = bf16[16,512]{1,0:T(8,128)(2,1)} fusion(bf16[16,256]{1,0:T(8,128)(2,1)S(1)} %copy-done.1, bf16[256,512]{1,0:T(8,128)(2,1)S(1)} %all_to_all.14), kind=kOutput, calls=%fused_computation | convolution fusion | flops 4202496 | bytes 286720 | tf_op jit(solution)/shard_map/dot_general | solution.py:260
Async XLA Ops:
  1.6 14.5 %all-to-all-start = ((bf16[32,16,128]{2,1,0:T(8,128)(2,1)}), bf16[32,16,128]{2,1,0:T(8,128)(2,1)S(1)}, u32[]{:S(2)}, u32[]{:S(2)}) async-start(bf16[32,16,128]{2,1,0:T(8,128)(2,1)} %get-tuple-element.11), calls=%async_computation | async-start | bytes 262144 | tf_op jit(solution)/shard_map/all_to_all | solution.py:221
  9.2 0.7 %copy-start = (s32[256]{0:T(256)S(1)}, s32[256]{0:T(256)}, u32[]{:S(2)}) copy-start(s32[256]{0:T(256)} %child_parent_in.1) | copy-start | bytes 3076
  16.0 24.4 %copy-start.1 = (bf16[16,256]{1,0:T(8,128)(2,1)S(1)}, bf16[16,256]{1,0:T(8,128)(2,1)}, u32[]{:S(2)}) copy-start(bf16[16,256]{1,0:T(8,128)(2,1)} %get-tuple-element.9) | copy-start | bytes 24580

commit v4 on v3

--- a/solution.py
+++ b/solution.py
@@ -15,8 +15,7 @@
 LOG2_E = 1.4426950408889634
 NEAR = 6
 STAGES = (0, 1, 2, 3), (4, 5, 6, 7)
-WAVES = (0, 2), (2, 5), (5, 8)
-LATE = {}
+CUTS = (0, 3, 6, 8)
 
 
 def pack_kernel(parents, child_count, place, child_parent, parent_len, queries, new_kv, packets, pick, seen):
@@ -133,24 +132,25 @@
     parts = out.shape[0] // slots
     near_count = near.shape[0]
     get_far = pltpu.make_async_copy(cache_hbm.at[pl.ds(near_count, parents - near_count)], far, far_sem)
+    bounds = [(cut * part, after * part) for cut, after in zip(CUTS, CUTS[1:])]
     get_weight = [
         pltpu.make_async_copy(
-            weight_hbm.at[:, pl.ds(i * part, part)], weight.at[:, pl.ds(i * part, part)], weight_sems.at[i]
+            weight_hbm.at[:, pl.ds(cut, after - cut)], weight.at[:, pl.ds(cut, after - cut)], weight_sems.at[i]
         )
-        for i in range(parts)
+        for i, (cut, after) in enumerate(bounds)
     ]
     get_plan = pltpu.make_async_copy(plan_in, plan, plan_sem)
     get_plan.start()
     get_far.start()
-    for i in range(*WAVES[0]):
-        get_weight[i].start()
+    for copy in get_weight:
+        copy.start(priority=1)
     get_plan.wait()
     heads[...] = jnp.zeros_like(heads)
 
     def block(p):
         return (near, p) if p < near_count else (far, p - near_count)
 
-    for stage, some in enumerate(STAGES):
+    for some in STAGES:
         if some[-1] == parents - 1:
             get_far.wait()
         places = [[plan[p * GROUP + k] for k in range(GROUP)] for p in some]
@@ -163,9 +163,6 @@
         for spots, result in zip(places, results):
             for k, at in enumerate(spots):
                 heads[pl.ds(pl.multiple_of(at * group, group), group), :] = result[k * group : (k + 1) * group]
-        for i in range(*WAVES[stage + 1]):
-            get_weight[i].start()
-
     def one(keys, at):
         return attend([[packets[at]]], [keys[:, :head_size]], [keys[:, head_size:]], group)[0]
 
@@ -188,9 +185,8 @@
         [heads[pl.ds(i, slots, stride=group), :].astype(jnp.bfloat16) for i in range(group)], axis=1
     )
     for i in range(parts):
-        get_weight[i].wait()
-        for j in range(*LATE.get(i, (0, 0))):
-            get_weight[j].start()
+        if i in CUTS:
+            get_weight[CUTS.index(i)].wait()
         out[i * slots : (i + 1) * slots, :] = jnp.dot(
             left, weight[:, i * part : (i + 1) * part], preferred_element_type=jnp.float32
         ).astype(out.dtype)
@@ -251,7 +247,7 @@
             pltpu.VMEM(((slots + 1) * group, head_size), jnp.float32),
             pltpu.SemaphoreType.DMA,
             pltpu.SemaphoreType.DMA,
-            pltpu.SemaphoreType.DMA((tps,)),
+            pltpu.SemaphoreType.DMA((len(CUTS) - 1,)),
         ],
         compiler_params=pltpu.CompilerParams(vmem_limit_bytes=50 * MIB),
     )(plan, packets, near, caches, out_weight)

time: 41.5 us -> 41.1 us (level)
  Pallas kernels: 8.87 us -> 8.4 us
    pallas_call x1, Pallas kernels: 4.81 us -> 4.34 us  [shards(): pl.pallas_call(functools.partial(attend_kernel, parents), out_shape=jax.S...]
where the time goes in v4:
time: 41.1 us; the launch traced here: 40.7 us
  blocking collectives  19.4 us (47%)
  Pallas kernels  8.4 us (20%)
  starting transfers between devices  7.58 us (18%)
  waiting for transfers between devices  3.68 us (9%)
  local copies, waits for them, and re-layouts  0.88 us (2%)
  matrix products  0.76 us (2%)
    all_to_all x1, blocking collectives, shards(): lax.all_to_all(partial, ('tp', 'rep'), split_axis=0, concat_axis=0, tiled...  19.4 us
    all_to_all x1, starting transfers between devices, shards(): lax.all_to_all(packets, 'rep', split_axis=0, concat_axis=0, tiled=True)  7.58 us
    pallas_call x1, Pallas kernels, shards(): pl.pallas_call(functools.partial(attend_kernel, parents), out_shape=jax.S...  4.34 us
    all_to_all x1, waiting for transfers between devices, shards(): lax.all_to_all(packets, 'rep', split_axis=0, concat_axis=0, tiled=True)  3.68 us
    pallas_call x1, Pallas kernels, shards(): pl.pallas_call(functools.partial(ahead_kernel, parents, child_count, slot...  2.5 us
    pallas_call x1, Pallas kernels, shards(): pl.pallas_call(functools.partial(pack_kernel, parents, child_count), out_...  1.56 us
  transfers between devices with their start and end apart: 1, of which 1 were waited for; matrix products, arithmetic and copies ran while one was open for 0% of the time, Pallas kernels for 6%

profile of v4, /device:TPU:1, one launch (start us, length us, event | category | flops | bytes accessed | tf_op | source)
XLA Modules:
  0.0 40.7 jit_solution(12041147779717970171)
XLA Ops:
  0.0 1.6 %shard_map.64 = (bf16[32,16,128]{2,1,0:T(8,128)(2,1)}, bf16[16,256]{1,0:T(8,128)(2,1)}) custom-call(s32[1]{0:T(128)} %bitcast.place, s32[256]{0:T(256)} %child_parent_in.1, s32[128]{0:T(128)} %parent_len.1, bf16[16,8,128]{2,1,0:T(8,128)(2,1)} %queries.1, bf16[16,256]{1,0:T(8,128)(2,1)} %bitcast.7), custom_call_target="tpu_custom_call" | custom-call | tf_op jit(solution)/shard_map/pallas_call | solution.py:207
  1.6 7.6 %all-to-all-start = ((bf16[32,16,128]{2,1,0:T(8,128)(2,1)}), bf16[32,16,128]{2,1,0:T(8,128)(2,1)S(1)}, u32[]{:S(2)}, u32[]{:S(2)}) async-start(bf16[32,16,128]{2,1,0:T(8,128)(2,1)} %get-tuple-element.11), calls=%async_computation | async-start | bytes 262144 | tf_op jit(solution)/shard_map/all_to_all | solution.py:217
  9.2 0.0 copy-start
  9.2 0.7 %copy-done = s32[256]{0:T(256)S(1)} copy-done((s32[256]{0:T(256)S(1)}, s32[256]{0:T(256)}, u32[]{:S(2)}) %copy-start) | copy-done | bytes 1048
  9.8 2.5 %shard_map.65 = (bf16[6,1024,256]{2,1,0:T(8,128)(2,1)S(1)}, s32[128]{0:T(128)S(1)}) custom-call(s32[1]{0:T(128)} %bitcast.place, s32[256]{0:T(256)S(1)} %copy-done, bf16[8,1024,256]{2,1,0:T(8,128)(2,1)} %bitcast.5), custom_call_target="tpu_custom_call" | custom-call | bytes 8388608 | tf_op jit(solution)/shard_map/pallas_call | solution.py:220
  12.3 3.7 %all-to-all-done.packets = bf16[32,16,128]{2,1,0:T(8,128)(2,1)S(1)} async-done(((bf16[32,16,128]{2,1,0:T(8,128)(2,1)}), bf16[32,16,128]{2,1,0:T(8,128)(2,1)S(1)}, u32[]{:S(2)}, u32[]{:S(2)}) %all-to-all-start) | async-done | bytes 131104 | tf_op jit(solution)/shard_map/all_to_all | solution.py:217
  16.0 0.0 copy-start.1
  16.0 4.3 %shard_map.66 = bf16[256,512]{1,0:T(8,128)(2,1)S(1)} custom-call(s32[128]{0:T(128)S(1)} %get-tuple-element.10.plan_in, bf16[32,16,128]{2,1,0:T(8,128)(2,1)S(1)} %all-to-all-done.packets, bf16[6,1024,256]{2,1,0:T(8,128)(2,1)S(1)} %get-tuple-element.12.near, bf16[8,1024,256]{2,1,0:T(8,128)(2,1)} %bitcast.6, bf16[1024,4096]{1,0:T(8,128)(2,1)} %weight_hbm.1), custom_call_target="tpu_custom_call" | custom-call | tf_op jit(solution)/shard_map/pallas_call | solution.py:238
  20.4 0.1 all_to_all.12
  20.5 19.4 %all_to_all.17 = bf16[128,2,512]{2,1,0:T(2,128)(2,1)S(1)} all-to-all(bf16[128,2,512]{2,1,0:T(2,128)(2,1)S(1)} %all_to_all.12), channel_id=1, replica_groups=mesh['rep'=16,'tp'=8] {'tp','rep'}, dimensions={0} | all-to-all | bytes 524288 | tf_op jit(solution)/shard_map/all_to_all | solution.py:255
  39.9 0.1 all_to_all.14
  40.0 0.0 copy-done.1
  40.0 0.8 %convolution_convert_fusion = bf16[16,512]{1,0:T(8,128)(2,1)} fusion(bf16[16,256]{1,0:T(8,128)(2,1)S(1)} %copy-done.1, bf16[256,512]{1,0:T(8,128)(2,1)S(1)} %all_to_all.14), kind=kOutput, calls=%fused_computation | convolution fusion | flops 4202496 | bytes 286720 | tf_op jit(solution)/shard_map/dot_general | solution.py:256
Async XLA Ops:
  1.6 14.5 %all-to-all-start = ((bf16[32,16,128]{2,1,0:T(8,128)(2,1)}), bf16[32,16,128]{2,1,0:T(8,128)(2,1)S(1)}, u32[]{:S(2)}, u32[]{:S(2)}) async-start(bf16[32,16,128]{2,1,0:T(8,128)(2,1)} %get-tuple-element.11), calls=%async_computation | async-start | bytes 262144 | tf_op jit(solution)/shard_map/all_to_all | solution.py:217
  9.2 0.7 %copy-start = (s32[256]{0:T(256)S(1)}, s32[256]{0:T(256)}, u32[]{:S(2)}) copy-start(s32[256]{0:T(256)} %child_parent_in.1) | copy-start | bytes 3076
  16.0 23.9 %copy-start.1 = (bf16[16,256]{1,0:T(8,128)(2,1)S(1)}, bf16[16,256]{1,0:T(8,128)(2,1)}, u32[]{:S(2)}) copy-start(bf16[16,256]{1,0:T(8,128)(2,1)} %get-tuple-element.9) | copy-start | bytes 24580

commit v5 on v4

--- a/solution.py
+++ b/solution.py
@@ -8,7 +8,9 @@
 from jax.sharding import PartitionSpec as P
 
 MOST = 2
-ROWS = 16
+ROWS = 8
+BLOCKS = MOST + 1
+EXTRA_ROWS = 4
 GROUP = 8
 COUNTS, EXTRAS, EXTRA_COUNT, PLAN = 64, 80, 127, 128
 MIB = 1024 * 1024
@@ -18,14 +20,15 @@
 CUTS = (0, 3, 6, 8)
 
 
-def pack_kernel(parents, child_count, place, child_parent, parent_len, queries, new_kv, packets, pick, seen):
+def pack_kernel(parents, child_count, place, child_parent, parent_len, queries, new_kv, packets, pick, seen, tails):
     packets[...] = jnp.zeros_like(packets)
-    holders = packets.shape[0] // MOST
+    tails[...] = jnp.zeros_like(tails)
+    holders = packets.shape[0] // BLOCKS
     for h in range(holders):
         seen[h] = 0
     head_size = queries.shape[-1]
     base = place[0] * child_count
-    row = lax.broadcasted_iota(jnp.int32, (8, head_size), 0)
+    row = lax.broadcasted_iota(jnp.int32, (ROWS, head_size), 0)
     pick_row = lax.broadcasted_iota(jnp.int32, pick.shape, 0)
     pick_col = lax.broadcasted_iota(jnp.int32, pick.shape, 1) % (holders * MOST)
     chosen = jnp.zeros(pick.shape, jnp.bool_)
@@ -38,12 +41,15 @@
         fresh = new_kv[c : c + 1, :].astype(jnp.float32)
         length = parent_len[parent]
         high, low = lax.div(length, 32).astype(jnp.float32), lax.rem(length, 32).astype(jnp.float32)
-        tail = jnp.where(row == 0, fresh[:, :head_size], fresh[:, head_size:])
-        tail = jnp.where(row < 2, tail, jnp.where(row == 2, high, low))
-        packet = jnp.concatenate([queries[c].astype(jnp.float32), tail], axis=0)
-        packets[slot] = packet.astype(packets.dtype)
+        at = row - rank * EXTRA_ROWS
+        tail = jnp.where(at == 0, fresh[:, :head_size], fresh[:, head_size:])
+        tail = jnp.where(at < 2, tail, jnp.where(at == 2, high, low))
+        tails[holder] = jnp.where((at >= 0) & (at < EXTRA_ROWS), tail, tails[holder])
+        packets[holder * BLOCKS + rank] = queries[c]
         chosen = chosen | ((pick_row == c) & (pick_col == slot))
     pick[...] = jnp.where(chosen, 1.0, 0.0).astype(pick.dtype)
+    for h in range(holders):
+        packets[h * BLOCKS + MOST] = tails[h].astype(packets.dtype)
 
 
 def ahead_kernel(
@@ -54,51 +60,54 @@
     get_parent = pltpu.make_async_copy(child_parent_in, child_parent, parent_sem)
     get_parent.start()
     get_near.start()
-    base = place[0] * parents
     for i in range(parents * GROUP):
         plan[i] = slots
     for p in range(parents):
         plan[COUNTS + p] = 0
     get_parent.wait()
+    held = slots // MOST * parents
     count = jnp.int32(0)
     for r in range(slots // MOST):
-        rank = jnp.int32(0)
         for c in range(child_count):
-            local = child_parent[r * child_count + c] - base
-            hits[count] = (r * MOST + rank) * parents + local
-            hit = ((local >= 0) & (local < parents)).astype(jnp.int32)
-            count = count + hit
-            rank = rank + hit
-
-    def sort(i, extra):
-        slot, local = lax.div(hits[i], parents), lax.rem(hits[i], parents)
+            parent = child_parent[r * child_count + c]
+            hits[count] = parent + r * held
+            count = count + (lax.div(parent, parents) == place[0]).astype(jnp.int32)
+
+    def sort(i, carry):
+        extra, last, rank = carry
+        rep, local = lax.div(hits[i], held), lax.rem(hits[i], parents)
+        rank = jnp.where(rep == last, rank + 1, 0)
+        slot = rep * MOST + rank
         before = plan[COUNTS + local]
         plan[COUNTS + local] = before + 1
         fits = before < GROUP
-
-        @pl.when(fits)
-        def _():
-            plan[local * GROUP + before] = slot
-
-        @pl.when(jnp.logical_not(fits))
-        def _():
-            plan[EXTRAS + extra] = hits[i]
-
-        return extra + jnp.where(fits, 0, 1)
-
-    plan[EXTRA_COUNT] = lax.fori_loop(0, count, sort, jnp.int32(0))
+        plan[jnp.where(fits, local * GROUP + before, EXTRAS + extra)] = jnp.where(fits, slot, slot * parents + local)
+        return extra + jnp.where(fits, 0, 1), rep, rank
+
+    start = (jnp.int32(0), jnp.int32(-1), jnp.int32(0))
+    plan[EXTRA_COUNT] = lax.fori_loop(0, count, sort, start)[0]
     get_near.wait()
+
+
+def unpack(packets, slot):
+    holder, rank = lax.div(slot, MOST), lax.rem(slot, MOST)
+    query = packets[holder * BLOCKS + rank].astype(jnp.float32)
+    tail = packets[holder * BLOCKS + MOST].astype(jnp.float32)
+    rows = [
+        jnp.where(rank == 0, tail[i : i + 1], tail[i + EXTRA_ROWS : i + EXTRA_ROWS + 1]) for i in range(EXTRA_ROWS)
+    ]
+    return query, rows
 
 
 def attend(packet_lists, keys, values, group):
     head_size = keys[0].shape[1]
     scale = head_size ** (-0.5) * LOG2_E
 
-    def row_of(packet, i):
-        return jnp.broadcast_to(packet[group + i : group + i + 1], (group, head_size))
-
-    wide = [[x.astype(jnp.float32) for x in packets] for packets in packet_lists]
-    query = [jnp.concatenate([w[:group] for w in ws], axis=0) for ws in wide]
+    def row_of(child, i):
+        return jnp.broadcast_to(child[1][i], (group, head_size))
+
+    wide = packet_lists
+    query = [jnp.concatenate([w[0] for w in ws], axis=0) for ws in wide]
     scores = [
         lax.dot_general(q.astype(jnp.bfloat16), k, (((1,), (1,)), ((), ())), preferred_element_type=jnp.float32)
         for q, k in zip(query, keys)
@@ -126,8 +135,8 @@
     parents, plan_in, packets, near, cache_hbm, weight_hbm, out,
     plan, far, weight, heads, plan_sem, far_sem, weight_sems,
 ):
-    slots = packets.shape[0]
-    group, head_size = 8, packets.shape[-1]
+    slots = packets.shape[0] // BLOCKS * MOST
+    group, head_size = packets.shape[1:]
     part = out.shape[1]
     parts = out.shape[0] // slots
     near_count = near.shape[0]
@@ -155,7 +164,7 @@
             get_far.wait()
         places = [[plan[p * GROUP + k] for k in range(GROUP)] for p in some]
         results = attend(
-            [[packets[jnp.minimum(at, slots - 1)] for at in spots] for spots in places],
+            [[unpack(packets, jnp.minimum(at, slots - 1)) for at in spots] for spots in places],
             [block(p)[0][block(p)[1], :, :head_size] for p in some],
             [block(p)[0][block(p)[1], :, head_size:] for p in some],
             group,
@@ -164,7 +173,7 @@
             for k, at in enumerate(spots):
                 heads[pl.ds(pl.multiple_of(at * group, group), group), :] = result[k * group : (k + 1) * group]
     def one(keys, at):
-        return attend([[packets[at]]], [keys[:, :head_size]], [keys[:, head_size:]], group)[0]
+        return attend([[unpack(packets, at)]], [keys[:, :head_size]], [keys[:, head_size:]], group)[0]
 
     def extra(i, carry):
         at, local = lax.div(plan[EXTRAS + i], parents), lax.rem(plan[EXTRAS + i], parents)
@@ -207,12 +216,12 @@
     packets, pick = pl.pallas_call(
         functools.partial(pack_kernel, parents, child_count),
         out_shape=(
-            jax.ShapeDtypeStruct((slots, ROWS, head_size), jnp.bfloat16),
+            jax.ShapeDtypeStruct((reps * BLOCKS, ROWS, head_size), jnp.bfloat16),
             jax.ShapeDtypeStruct((child_count, tps * slots), jnp.bfloat16),
         ),
         in_specs=[smem, smem, smem, vmem, vmem],
         out_specs=(vmem, vmem),
-        scratch_shapes=[pltpu.SMEM((reps,), jnp.int32)],
+        scratch_shapes=[pltpu.SMEM((reps,), jnp.int32), pltpu.VMEM((reps, ROWS, head_size), jnp.float32)],
     )(place, child_parent, parent_len, queries, new_kv.reshape(child_count, width))
     packets = lax.all_to_all(packets, "rep", split_axis=0, concat_axis=0, tiled=True)
 

time: 41.1 us -> 41 us (level)
  no operation moved by 1% of the time
where the time goes in v5:
time: 41 us; the launch traced here: 40.6 us
  blocking collectives  19.4 us (47%)
  Pallas kernels  8.4 us (20%)
  starting transfers between devices  7.59 us (19%)
  waiting for transfers between devices  3.54 us (9%)
  local copies, waits for them, and re-layouts  0.88 us (2%)
  matrix products  0.76 us (2%)
    all_to_all x1, blocking collectives, shards(): lax.all_to_all(partial, ('tp', 'rep'), split_axis=0, concat_axis=0, tiled...  19.4 us
    all_to_all x1, starting transfers between devices, shards(): lax.all_to_all(packets, 'rep', split_axis=0, concat_axis=0, tiled=True)  7.59 us
    pallas_call x1, Pallas kernels, shards(): pl.pallas_call(functools.partial(attend_kernel, parents), out_shape=jax.S...  4.34 us
    all_to_all x1, waiting for transfers between devices, shards(): lax.all_to_all(packets, 'rep', split_axis=0, concat_axis=0, tiled=True)  3.54 us
    pallas_call x1, Pallas kernels, shards(): pl.pallas_call(functools.partial(ahead_kernel, parents, child_count, slot...  2.5 us
    pallas_call x1, Pallas kernels, shards(): pl.pallas_call(functools.partial(pack_kernel, parents, child_count), out_...  1.56 us
  transfers between devices with their start and end apart: 1, of which 1 were waited for; matrix products, arithmetic and copies ran while one was open for 0% of the time, Pallas kernels for 6%

profile of v5, /device:TPU:1, one launch (start us, length us, event | category | flops | bytes accessed | tf_op | source)
XLA Modules:
  0.0 40.6 jit_solution(8109552342526572983)
XLA Ops:
  0.0 1.6 %shard_map.64 = (bf16[48,8,128]{2,1,0:T(8,128)(2,1)}, bf16[16,256]{1,0:T(8,128)(2,1)}) custom-call(s32[1]{0:T(128)} %bitcast.place, s32[256]{0:T(256)} %child_parent_in.1, s32[128]{0:T(128)} %parent_len.1, bf16[16,8,128]{2,1,0:T(8,128)(2,1)} %queries.1, bf16[16,256]{1,0:T(8,128)(2,1)} %bitcast.7), custom_call_target="tpu_custom_call" | custom-call | tf_op jit(solution)/shard_map/pallas_call | solution.py:216
  1.6 7.6 %all-to-all-start = ((bf16[48,8,128]{2,1,0:T(8,128)(2,1)}), bf16[48,8,128]{2,1,0:T(8,128)(2,1)S(1)}, u32[]{:S(2)}, u32[]{:S(2)}) async-start(bf16[48,8,128]{2,1,0:T(8,128)(2,1)} %get-tuple-element.11), calls=%async_computation | async-start | bytes 196608 | tf_op jit(solution)/shard_map/all_to_all | solution.py:226
  9.2 0.0 copy-start
  9.2 0.7 %copy-done = s32[256]{0:T(256)S(1)} copy-done((s32[256]{0:T(256)S(1)}, s32[256]{0:T(256)}, u32[]{:S(2)}) %copy-start) | copy-done | bytes 1048
  9.8 2.5 %shard_map.65 = (bf16[6,1024,256]{2,1,0:T(8,128)(2,1)S(1)}, s32[128]{0:T(128)S(1)}) custom-call(s32[1]{0:T(128)} %bitcast.place, s32[256]{0:T(256)S(1)} %copy-done, bf16[8,1024,256]{2,1,0:T(8,128)(2,1)} %bitcast.5), custom_call_target="tpu_custom_call" | custom-call | bytes 8388608 | tf_op jit(solution)/shard_map/pallas_call | solution.py:229
  12.3 3.5 %all-to-all-done.packets = bf16[48,8,128]{2,1,0:T(8,128)(2,1)S(1)} async-done(((bf16[48,8,128]{2,1,0:T(8,128)(2,1)}), bf16[48,8,128]{2,1,0:T(8,128)(2,1)S(1)}, u32[]{:S(2)}, u32[]{:S(2)}) %all-to-all-start) | async-done | bytes 98336 | tf_op jit(solution)/shard_map/all_to_all | solution.py:226
  15.9 0.0 copy-start.1
  15.9 4.3 %shard_map.66 = bf16[256,512]{1,0:T(8,128)(2,1)S(1)} custom-call(s32[128]{0:T(128)S(1)} %get-tuple-element.10.plan_in, bf16[48,8,128]{2,1,0:T(8,128)(2,1)S(1)} %all-to-all-done.packets, bf16[6,1024,256]{2,1,0:T(8,128)(2,1)S(1)} %get-tuple-element.12.near, bf16[8,1024,256]{2,1,0:T(8,128)(2,1)} %bitcast.6, bf16[1024,4096]{1,0:T(8,128)(2,1)} %weight_hbm.1), custom_call_target="tpu_custom_call" | custom-call | tf_op jit(solution)/shard_map/pallas_call | solution.py:247
  20.2 0.1 all_to_all.12
  20.3 19.4 %all_to_all.17 = bf16[128,2,512]{2,1,0:T(2,128)(2,1)S(1)} all-to-all(bf16[128,2,512]{2,1,0:T(2,128)(2,1)S(1)} %all_to_all.12), channel_id=1, replica_groups=mesh['rep'=16,'tp'=8] {'tp','rep'}, dimensions={0} | all-to-all | bytes 524288 | tf_op jit(solution)/shard_map/all_to_all | solution.py:264
  39.7 0.1 all_to_all.14
  39.8 0.0 copy-done.1
  39.9 0.8 %convolution_convert_fusion = bf16[16,512]{1,0:T(8,128)(2,1)} fusion(bf16[16,256]{1,0:T(8,128)(2,1)S(1)} %copy-done.1, bf16[256,512]{1,0:T(8,128)(2,1)S(1)} %all_to_all.14), kind=kOutput, calls=%fused_computation | convolution fusion | flops 4202496 | bytes 286720 | tf_op jit(solution)/shard_map/dot_general | solution.py:265
Async XLA Ops:
  1.6 14.3 %all-to-all-start = ((bf16[48,8,128]{2,1,0:T(8,128)(2,1)}), bf16[48,8,128]{2,1,0:T(8,128)(2,1)S(1)}, u32[]{:S(2)}, u32[]{:S(2)}) async-start(bf16[48,8,128]{2,1,0:T(8,128)(2,1)} %get-tuple-element.11), calls=%async_computation | async-start | bytes 196608 | tf_op jit(solution)/shard_map/all_to_all | solution.py:226
  9.2 0.7 %copy-start = (s32[256]{0:T(256)S(1)}, s32[256]{0:T(256)}, u32[]{:S(2)}) copy-start(s32[256]{0:T(256)} %child_parent_in.1) | copy-start | bytes 3076
  15.9 24.0 %copy-start.1 = (bf16[16,256]{1,0:T(8,128)(2,1)S(1)}, bf16[16,256]{1,0:T(8,128)(2,1)}, u32[]{:S(2)}) copy-start(bf16[16,256]{1,0:T(8,128)(2,1)} %get-tuple-element.9) | copy-start | bytes 24580

commit v6 on v5

--- a/solution.py
+++ b/solution.py
@@ -17,7 +17,8 @@
 LOG2_E = 1.4426950408889634
 NEAR = 6
 STAGES = (0, 1, 2, 3), (4, 5, 6, 7)
-CUTS = (0, 3, 6, 8)
+CUTS = (0, 4, 6, 8)
+WIDE = 2
 
 
 def pack_kernel(parents, child_count, place, child_parent, parent_len, queries, new_kv, packets, pick, seen, tails):
@@ -193,12 +194,13 @@
     left = jnp.concatenate(
         [heads[pl.ds(i, slots, stride=group), :].astype(jnp.bfloat16) for i in range(group)], axis=1
     )
-    for i in range(parts):
-        if i in CUTS:
-            get_weight[CUTS.index(i)].wait()
-        out[i * slots : (i + 1) * slots, :] = jnp.dot(
-            left, weight[:, i * part : (i + 1) * part], preferred_element_type=jnp.float32
-        ).astype(out.dtype)
+    for copy, (cut, after) in zip(get_weight, bounds):
+        copy.wait()
+        for low in range(cut, after, WIDE * part):
+            sums = jnp.dot(left, weight[:, low : low + WIDE * part], preferred_element_type=jnp.float32).astype(out.dtype)
+            for i in range(WIDE):
+                first = (low // part + i) * slots
+                out[first : first + slots, :] = sums[:, i * part : (i + 1) * part]
 
 
 def shards(queries, new_kv, parent_cache, parent_len, child_parent, out_weight):

time: 41 us -> 40.9 us (level)
  no operation moved by 1% of the time
where the time goes in v6:
time: 40.9 us; the launch traced here: 40.6 us
  blocking collectives  19.4 us (47%)
  Pallas kernels  8.39 us (21%)
  starting transfers between devices  7.59 us (19%)
  waiting for transfers between devices  3.54 us (9%)
  local copies, waits for them, and re-layouts  0.88 us (2%)
  matrix products  0.76 us (2%)
    all_to_all x1, blocking collectives, shards(): lax.all_to_all(partial, ('tp', 'rep'), split_axis=0, concat_axis=0, tiled...  19.4 us
    all_to_all x1, starting transfers between devices, shards(): lax.all_to_all(packets, 'rep', split_axis=0, concat_axis=0, tiled=True)  7.59 us
    pallas_call x1, Pallas kernels, shards(): pl.pallas_call(functools.partial(attend_kernel, parents), out_shape=jax.S...  4.33 us
    all_to_all x1, waiting for transfers between devices, shards(): lax.all_to_all(packets, 'rep', split_axis=0, concat_axis=0, tiled=True)  3.54 us
    pallas_call x1, Pallas kernels, shards(): pl.pallas_call(functools.partial(ahead_kernel, parents, child_count, slot...  2.5 us
    pallas_call x1, Pallas kernels, shards(): pl.pallas_call(functools.partial(pack_kernel, parents, child_count), out_...  1.56 us
  transfers between devices with their start and end apart: 1, of which 1 were waited for; matrix products, arithmetic and copies ran while one was open for 0% of the time, Pallas kernels for 6%

profile of v6, /device:TPU:1, one launch (start us, length us, event | category | flops | bytes accessed | tf_op | source)
XLA Modules:
  0.0 40.6 jit_solution(9641016700626226979)
XLA Ops:
  0.0 1.6 %shard_map.64 = (bf16[48,8,128]{2,1,0:T(8,128)(2,1)}, bf16[16,256]{1,0:T(8,128)(2,1)}) custom-call(s32[1]{0:T(128)} %bitcast.place, s32[256]{0:T(256)} %child_parent_in.1, s32[128]{0:T(128)} %parent_len.1, bf16[16,8,128]{2,1,0:T(8,128)(2,1)} %queries.1, bf16[16,256]{1,0:T(8,128)(2,1)} %bitcast.7), custom_call_target="tpu_custom_call" | custom-call | tf_op jit(solution)/shard_map/pallas_call | solution.py:218
  1.6 7.6 %all-to-all-start = ((bf16[48,8,128]{2,1,0:T(8,128)(2,1)}), bf16[48,8,128]{2,1,0:T(8,128)(2,1)S(1)}, u32[]{:S(2)}, u32[]{:S(2)}) async-start(bf16[48,8,128]{2,1,0:T(8,128)(2,1)} %get-tuple-element.11), calls=%async_computation | async-start | bytes 196608 | tf_op jit(solution)/shard_map/all_to_all | solution.py:228
  9.2 0.0 copy-start
  9.2 0.7 %copy-done = s32[256]{0:T(256)S(1)} copy-done((s32[256]{0:T(256)S(1)}, s32[256]{0:T(256)}, u32[]{:S(2)}) %copy-start) | copy-done | bytes 1048
  9.8 2.5 %shard_map.65 = (bf16[6,1024,256]{2,1,0:T(8,128)(2,1)S(1)}, s32[128]{0:T(128)S(1)}) custom-call(s32[1]{0:T(128)} %bitcast.place, s32[256]{0:T(256)S(1)} %copy-done, bf16[8,1024,256]{2,1,0:T(8,128)(2,1)} %bitcast.5), custom_call_target="tpu_custom_call" | custom-call | bytes 8388608 | tf_op jit(solution)/shard_map/pallas_call | solution.py:231
  12.3 3.5 %all-to-all-done.packets = bf16[48,8,128]{2,1,0:T(8,128)(2,1)S(1)} async-done(((bf16[48,8,128]{2,1,0:T(8,128)(2,1)}), bf16[48,8,128]{2,1,0:T(8,128)(2,1)S(1)}, u32[]{:S(2)}, u32[]{:S(2)}) %all-to-all-start) | async-done | bytes 98336 | tf_op jit(solution)/shard_map/all_to_all | solution.py:228
  15.9 0.0 copy-start.1
  15.9 4.3 %shard_map.66 = bf16[256,512]{1,0:T(8,128)(2,1)S(1)} custom-call(s32[128]{0:T(128)S(1)} %get-tuple-element.10.plan_in, bf16[48,8,128]{2,1,0:T(8,128)(2,1)S(1)} %all-to-all-done.packets, bf16[6,1024,256]{2,1,0:T(8,128)(2,1)S(1)} %get-tuple-element.12.near, bf16[8,1024,256]{2,1,0:T(8,128)(2,1)} %bitcast.6, bf16[1024,4096]{1,0:T(8,128)(2,1)} %weight_hbm.1), custom_call_target="tpu_custom_call" | custom-call | tf_op jit(solution)/shard_map/pallas_call | solution.py:249
  20.2 0.1 all_to_all.12
  20.3 19.4 %all_to_all.17 = bf16[128,2,512]{2,1,0:T(2,128)(2,1)S(1)} all-to-all(bf16[128,2,512]{2,1,0:T(2,128)(2,1)S(1)} %all_to_all.12), channel_id=1, replica_groups=mesh['rep'=16,'tp'=8] {'tp','rep'}, dimensions={0} | all-to-all | bytes 524288 | tf_op jit(solution)/shard_map/all_to_all | solution.py:266
  39.7 0.1 all_to_all.14
  39.8 0.0 copy-done.1
  39.8 0.8 %convolution_convert_fusion = bf16[16,512]{1,0:T(8,128)(2,1)} fusion(bf16[16,256]{1,0:T(8,128)(2,1)S(1)} %copy-done.1, bf16[256,512]{1,0:T(8,128)(2,1)S(1)} %all_to_all.14), kind=kOutput, calls=%fused_computation | convolution fusion | flops 4202496 | bytes 286720 | tf_op jit(solution)/shard_map/dot_general | solution.py:267
Async XLA Ops:
  1.6 14.3 %all-to-all-start = ((bf16[48,8,128]{2,1,0:T(8,128)(2,1)}), bf16[48,8,128]{2,1,0:T(8,128)(2,1)S(1)}, u32[]{:S(2)}, u32[]{:S(2)}) async-start(bf16[48,8,128]{2,1,0:T(8,128)(2,1)} %get-tuple-element.11), calls=%async_computation | async-start | bytes 196608 | tf_op jit(solution)/shard_map/all_to_all | solution.py:228
  9.2 0.7 %copy-start = (s32[256]{0:T(256)S(1)}, s32[256]{0:T(256)}, u32[]{:S(2)}) copy-start(s32[256]{0:T(256)} %child_parent_in.1) | copy-start | bytes 3076
  15.9 23.9 %copy-start.1 = (bf16[16,256]{1,0:T(8,128)(2,1)S(1)}, bf16[16,256]{1,0:T(8,128)(2,1)}, u32[]{:S(2)}) copy-start(bf16[16,256]{1,0:T(8,128)(2,1)} %get-tuple-element.9) | copy-start | bytes 24580

commit v7 on v6

--- a/solution.py
+++ b/solution.py
@@ -16,7 +16,7 @@
 MIB = 1024 * 1024
 LOG2_E = 1.4426950408889634
 NEAR = 6
-STAGES = (0, 1, 2, 3), (4, 5, 6, 7)
+STAGES = (0, 1, 2, 3, 4, 5), (6, 7)
 CUTS = (0, 4, 6, 8)
 WIDE = 2
 

time: 40.9 us -> 40.9 us (level)
  no operation moved by 1% of the time
where the time goes in v7:
time: 40.9 us; the launch traced here: 40.6 us
  blocking collectives  19.4 us (47%)
  Pallas kernels  8.39 us (21%)
  starting transfers between devices  7.58 us (19%)
  waiting for transfers between devices  3.54 us (9%)
  local copies, waits for them, and re-layouts  0.88 us (2%)
  matrix products  0.76 us (2%)
    all_to_all x1, blocking collectives, shards(): lax.all_to_all(partial, ('tp', 'rep'), split_axis=0, concat_axis=0, tiled...  19.4 us
    all_to_all x1, starting transfers between devices, shards(): lax.all_to_all(packets, 'rep', split_axis=0, concat_axis=0, tiled=True)  7.58 us
    pallas_call x1, Pallas kernels, shards(): pl.pallas_call(functools.partial(attend_kernel, parents), out_shape=jax.S...  4.33 us
    all_to_all x1, waiting for transfers between devices, shards(): lax.all_to_all(packets, 'rep', split_axis=0, concat_axis=0, tiled=True)  3.54 us
    pallas_call x1, Pallas kernels, shards(): pl.pallas_call(functools.partial(ahead_kernel, parents, child_count, slot...  2.5 us
    pallas_call x1, Pallas kernels, shards(): pl.pallas_call(functools.partial(pack_kernel, parents, child_count), out_...  1.57 us
  transfers between devices with their start and end apart: 1, of which 1 were waited for; matrix products, arithmetic and copies ran while one was open for 0% of the time, Pallas kernels for 6%

profile of v7, /device:TPU:1, one launch (start us, length us, event | category | flops | bytes accessed | tf_op | source)
XLA Modules:
  0.0 40.6 jit_solution(5599073984116401313)
XLA Ops:
  0.0 1.6 %shard_map.64 = (bf16[48,8,128]{2,1,0:T(8,128)(2,1)}, bf16[16,256]{1,0:T(8,128)(2,1)}) custom-call(s32[1]{0:T(128)} %bitcast.place, s32[256]{0:T(256)} %child_parent_in.1, s32[128]{0:T(128)} %parent_len.1, bf16[16,8,128]{2,1,0:T(8,128)(2,1)} %queries.1, bf16[16,256]{1,0:T(8,128)(2,1)} %bitcast.7), custom_call_target="tpu_custom_call" | custom-call | tf_op jit(solution)/shard_map/pallas_call | solution.py:218
  1.6 7.6 %all-to-all-start = ((bf16[48,8,128]{2,1,0:T(8,128)(2,1)}), bf16[48,8,128]{2,1,0:T(8,128)(2,1)S(1)}, u32[]{:S(2)}, u32[]{:S(2)}) async-start(bf16[48,8,128]{2,1,0:T(8,128)(2,1)} %get-tuple-element.11), calls=%async_computation | async-start | bytes 196608 | tf_op jit(solution)/shard_map/all_to_all | solution.py:228
  9.2 0.0 copy-start
  9.2 0.7 %copy-done = s32[256]{0:T(256)S(1)} copy-done((s32[256]{0:T(256)S(1)}, s32[256]{0:T(256)}, u32[]{:S(2)}) %copy-start) | copy-done | bytes 1048
  9.8 2.5 %shard_map.65 = (bf16[6,1024,256]{2,1,0:T(8,128)(2,1)S(1)}, s32[128]{0:T(128)S(1)}) custom-call(s32[1]{0:T(128)} %bitcast.place, s32[256]{0:T(256)S(1)} %copy-done, bf16[8,1024,256]{2,1,0:T(8,128)(2,1)} %bitcast.5), custom_call_target="tpu_custom_call" | custom-call | bytes 8388608 | tf_op jit(solution)/shard_map/pallas_call | solution.py:231
  12.3 3.5 %all-to-all-done.packets = bf16[48,8,128]{2,1,0:T(8,128)(2,1)S(1)} async-done(((bf16[48,8,128]{2,1,0:T(8,128)(2,1)}), bf16[48,8,128]{2,1,0:T(8,128)(2,1)S(1)}, u32[]{:S(2)}, u32[]{:S(2)}) %all-to-all-start) | async-done | bytes 98336 | tf_op jit(solution)/shard_map/all_to_all | solution.py:228
  15.9 0.0 copy-start.1
  15.9 4.3 %shard_map.66 = bf16[256,512]{1,0:T(8,128)(2,1)S(1)} custom-call(s32[128]{0:T(128)S(1)} %get-tuple-element.10.plan_in, bf16[48,8,128]{2,1,0:T(8,128)(2,1)S(1)} %all-to-all-done.packets, bf16[6,1024,256]{2,1,0:T(8,128)(2,1)S(1)} %get-tuple-element.12.near, bf16[8,1024,256]{2,1,0:T(8,128)(2,1)} %bitcast.6, bf16[1024,4096]{1,0:T(8,128)(2,1)} %weight_hbm.1), custom_call_target="tpu_custom_call" | custom-call | tf_op jit(solution)/shard_map/pallas_call | solution.py:249
  20.2 0.1 all_to_all.12
  20.3 19.4 %all_to_all.17 = bf16[128,2,512]{2,1,0:T(2,128)(2,1)S(1)} all-to-all(bf16[128,2,512]{2,1,0:T(2,128)(2,1)S(1)} %all_to_all.12), channel_id=1, replica_groups=mesh['rep'=16,'tp'=8] {'tp','rep'}, dimensions={0} | all-to-all | bytes 524288 | tf_op jit(solution)/shard_map/all_to_all | solution.py:266
  39.7 0.1 all_to_all.14
  39.8 0.0 copy-done.1
  39.8 0.8 %convolution_convert_fusion = bf16[16,512]{1,0:T(8,128)(2,1)} fusion(bf16[16,256]{1,0:T(8,128)(2,1)S(1)} %copy-done.1, bf16[256,512]{1,0:T(8,128)(2,1)S(1)} %all_to_all.14), kind=kOutput, calls=%fused_computation | convolution fusion | flops 4202496 | bytes 286720 | tf_op jit(solution)/shard_map/dot_general | solution.py:267
Async XLA Ops:
  1.6 14.3 %all-to-all-start = ((bf16[48,8,128]{2,1,0:T(8,128)(2,1)}), bf16[48,8,128]{2,1,0:T(8,128)(2,1)S(1)}, u32[]{:S(2)}, u32[]{:S(2)}) async-start(bf16[48,8,128]{2,1,0:T(8,128)(2,1)} %get-tuple-element.11), calls=%async_computation | async-start | bytes 196608 | tf_op jit(solution)/shard_map/all_to_all | solution.py:228
  9.2 0.7 %copy-start = (s32[256]{0:T(256)S(1)}, s32[256]{0:T(256)}, u32[]{:S(2)}) copy-start(s32[256]{0:T(256)} %child_parent_in.1) | copy-start | bytes 3076
  15.9 23.9 %copy-start.1 = (bf16[16,256]{1,0:T(8,128)(2,1)S(1)}, bf16[16,256]{1,0:T(8,128)(2,1)}, u32[]{:S(2)}) copy-start(bf16[16,256]{1,0:T(8,128)(2,1)} %get-tuple-element.9) | copy-start | bytes 24580
